TPU v7x, 256 devices: a whole 4x4x8 slice. The times are simulated.
256 devices in a mesh: lev: 16 (over z, y_hi), lon: 16 (over x, y_lo, core).
Axes of the slice: x: 4, y: 4 (y_hi: 2, y_lo: 2; y = y_hi * 2 + y_lo), z: 8, core: 2. Of those that a mesh axis runs over, the one named last changes fastest.
Arguments:
- field: bfloat16 [2, 144, 1536, 256], P(None, 'lev', 'lon'), may hold values from -6 to 6
- eof_basis: bfloat16 [144, 64], replicated, may hold values from -0.5 to 0.5
- band_of_mode: int32 [64], replicated, may hold values from 0 to 7
- coef_table: float32 [8, 256], replicated, may hold values from 0.02 to 0.24
Outputs:
- smoothed: bfloat16 [2, 144, 1536, 256], P(None, 'lev', 'lon')
All inputs are finite; a program needn't handle non-finite values.
Results may differ from a plain program's by a relative error of at most 0.013.
Values may be sent and summed in bfloat16 or wider, within the bound.
No kernel may reach another device: no remote copies, remote signals or barrier semaphores. Data moves between devices by JAX's collectives and lax.ppermute only.
A program may use at most 128 MiB of HBM per device.

v0:
```python
import jax
import jax.numpy as jnp
from jax import lax
from jax.sharding import PartitionSpec as P

STEPS = 8


def extended(cells, sides, width):
    for axis, dim in sides:
        count = lax.axis_size(axis)
        head = lax.slice_in_dim(cells, 0, width, axis=dim)
        tail = lax.slice_in_dim(cells, cells.shape[dim] - width, cells.shape[dim], axis=dim)
        cells = jnp.concatenate(
            [
                lax.ppermute(tail, axis, [(i, (i + 1) % count) for i in range(count)]),
                cells,
                lax.ppermute(head, axis, [((i + 1) % count, i) for i in range(count)]),
            ],
            axis=dim,
        )
    return cells


def lat_sum(u):
    upper = jnp.pad(u[..., 1:], ((0, 0), (0, 0), (0, 0), (0, 1)))
    lower = jnp.pad(u[..., :-1], ((0, 0), (0, 0), (0, 0), (1, 0)))
    return upper + lower


def on_device(field, eof_basis, band_of_mode, coef_table):
    groups = lax.axis_size("lev")
    position = lax.axis_index("lev")
    lev_dev = field.shape[1]
    owned = eof_basis.shape[1] // groups
    basis_rows = lax.dynamic_slice_in_dim(eof_basis, position * lev_dev, lev_dev, 0)
    columns = basis_rows
    modes = lax.psum_scatter(
        jnp.einsum("lk,mlxy->kmxy", columns, field, preferred_element_type=jnp.float32),
        "lev",
        scatter_dimension=0,
        tiled=True,
    ).astype(jnp.bfloat16)
    bands = lax.dynamic_slice_in_dim(band_of_mode, position * owned, owned, 0)
    onehot = (bands[:, None] == jnp.arange(coef_table.shape[0])[None, :]).astype(jnp.float32)
    kappa = jnp.dot(onehot, coef_table, precision=lax.Precision.HIGHEST)[:, None, None, :]
    u = modes.astype(jnp.float32)
    for step in range(STEPS):
        padded = extended(u.astype(jnp.bfloat16), (("lon", 2),), 1).astype(u.dtype)
        neighbours = padded[:, :, 2:] + padded[:, :, :-2] + lat_sum(u)
        u = u + kappa * (neighbours - 4.0 * u)
    diffused = u.astype(jnp.bfloat16)
    columns = basis_rows
    total = jnp.einsum(
        "lk,kmxy->mlxy",
        columns,
        lax.all_gather(diffused, "lev", axis=0, tiled=True),
        preferred_element_type=jnp.float32,
    )
    return total.astype(jnp.bfloat16)


def solution(mesh):
    return jax.shard_map(
        on_device,
        mesh=mesh,
        in_specs=(P(None, "lev", "lon", None), P(), P(), P()),
        out_specs=P(None, "lev", "lon", None),
        check_vma=False,
    )
```

profile of v0, /device:TPU:2, one launch (start us, length us, event | category | flops | bytes accessed | tf_op | source)
XLA Modules:
  0.0 465.4 jit_solution(3630992309290539793)
XLA Ops:
  6.5 1.2 copy-done
  7.7 7.1 %fusion.5 = f32[64,2,96,256]{3,0,2,1:T(8,128)} fusion(bf16[2,9,96,256]{3,2,1,0:T(8,128)(2,1)S(1)} %copy-done, bf16[144,64]{0,1:T(8,128)(2,1)} %param.5, s32[]{:T(128)S(6)} %select_n.6), kind=kOutput, calls=%fused_computation.3 | convolution fusion | flops 56623104 | bytes 13484036 | tf_op jit(solution)/shard_map/lk,mlxy->kmxy/dot_general | solution.py:39
  14.8 16.4 %copy.10 = f32[64,2,96,256]{3,2,1,0:T(8,128)} copy(f32[64,2,96,256]{3,0,2,1:T(8,128)} %fusion.5) | data formatting | bytes 25165824 | tf_op jit(solution)/shard_map/lk,mlxy->kmxy/dot_general | solution.py:39
  31.3 0.6 copy-done.3
  32.2 253.8 %reduce-scatter.2.cloned.1.call-done = f32[4,2,96,256]{3,2,1,0:T(8,128)} async-done(((f32[64,2,96,256]{3,2,1,0:T(8,128)}), f32[4,2,96,256]{3,2,1,0:T(8,128)}) %reduce-scatter.2.cloned.1.call-update) | async-done | bytes 786448 | tf_op jit(solution)/shard_map/reduce_scatter | solution.py:38
  286.0 1.2 convert_element_type.80
  287.3 2.6 collective-permute-start.1
  290.1 1.1 collective-permute-done
  291.4 1.6 fusion.63
  293.1 2.7 collective-permute-start.3
  296.1 1.0 collective-permute-done.2
  297.8 0.5 collective-permute-start.4
  298.3 2.3 collective-permute-start.5
  300.8 1.0 collective-permute-done.4
  302.5 0.5 collective-permute-start.6
  303.0 2.3 collective-permute-start.7
  305.6 1.0 collective-permute-done.6
  307.3 0.5 collective-permute-start.8
  307.7 2.3 collective-permute-start.9
  310.3 1.0 collective-permute-done.8
  312.0 0.5 collective-permute-start.10
  312.5 2.5 collective-permute-start.11
  315.3 0.8 collective-permute-done.10
  317.2 2.5 collective-permute-start.13
  320.0 1.0 collective-permute-done.12
  321.7 0.5 collective-permute-start.14
  322.2 2.3 collective-permute-start.15
  324.8 1.0 collective-permute-done.14
  326.0 1.2 fusion.14
  327.2 123.8 %all-gather.2.cloned.1.call-done = bf16[64,2,96,256]{3,2,1,0:T(8,128)(2,1)} async-done(((bf16[4,2,96,256]{3,2,1,0:T(8,128)(2,1)}), bf16[64,2,96,256]{3,2,1,0:T(8,128)(2,1)}) %all-gather.2.cloned.1.call-update) | async-done | bytes 6291472 | tf_op jit(solution)/shard_map/all_gather | solution.py:57
  451.0 6.3 %fusion.7 = bf16[2,9,96,256]{3,1,2,0:T(8,128)(2,1)S(1)} fusion(bf16[64,2,96,256]{3,2,1,0:T(8,128)(2,1)} %all-gather.2.cloned.1.call-done, bf16[144,64]{0,1:T(8,128)(2,1)S(1)} %copy-done.1, s32[]{:T(128)S(6)} %select_n.6), kind=kOutput, calls=%fused_computation.5 | convolution fusion | flops 57065472 | bytes 7192580 | tf_op jit(solution)/shard_map/lk,kmxy->mlxy/dot_general | solution.py:54
  457.3 1.2 copy.12
  (53 shorter events, 7.6 us)
Async XLA Ops:
  6.5 1.2 copy-start
  6.5 279.4 %reduce-scatter.2.cloned.1.call-start = ((), (), s32[]{:S(2)}) async-start(), calls=%async_computation.1 | async-start | bytes 13369344 | tf_op jit(solution)/shard_map/reduce_scatter | solution.py:38
  31.2 0.7 copy-start.3
  31.2 0.7 copy-start.2
  31.3 419.7 %all-gather.2.cloned.1.call-start = ((), (), s32[]{:S(2)}) async-start(), calls=%async_computation.2 | async-start | bytes 6684672 | tf_op jit(solution)/shard_map/all_gather | solution.py:57
  287.2 4.1 collective-permute-start
  287.3 4.0 collective-permute-start.1
  293.0 4.1 collective-permute-start.2
  293.1 4.0 collective-permute-start.3
  297.8 4.1 collective-permute-start.4
  298.3 3.7 collective-permute-start.5
  302.5 4.1 collective-permute-start.6
  303.0 3.7 collective-permute-start.7
  307.3 4.1 collective-permute-start.8
  307.7 3.7 collective-permute-start.9
  312.0 4.1 collective-permute-start.10
  312.5 3.9 collective-permute-start.11
  317.0 4.1 collective-permute-start.12
  317.2 3.9 collective-permute-start.13
  321.2 129.7 %copy-start.1 = (bf16[144,64]{0,1:T(8,128)(2,1)S(1)}, bf16[144,64]{0,1:T(8,128)(2,1)}, u32[]{:S(2)}) copy-start(bf16[144,64]{0,1:T(8,128)(2,1)} %param.5) | copy-start | bytes 55300
  321.7 4.1 collective-permute-start.14
  322.2 3.7 collective-permute-start.15
Sparse Core Ops, SparseCore 0:
  31.4 254.5 reduce-scatter.1
  327.3 123.6 all-gather.1
where the time goes:
time: 466 us; the launch traced here: 465 us
  waiting for transfers between devices  386 us (83%)
  starting transfers between devices  22.4 us (5%)
  local copies, waits for them, and re-layouts  21.8 us (5%)
  matrix products  13.7 us (3%)
  between operations  13.6 us (3%)
  other arithmetic  7.61 us (2%)
    reduce_scatter x1, waiting for transfers between devices, on_device(): lax.psum_scatter(jnp.einsum('lk,mlxy->kmxy', columns, field, preferred_el...  254 us
    all_gather x1, waiting for transfers between devices, on_device(): lax.all_gather(diffused, 'lev', axis=0, tiled=True)  124 us
    ppermute x8, starting transfers between devices, extended(): lax.ppermute(head, axis, [((i + 1) % count, i) for i in range(count)])  19.6 us
    dot_general x1, local copies, waits for them, and re-layouts, on_device(): jnp.einsum('lk,mlxy->kmxy', columns, field, preferred_element_type=jnp.fl...  16.4 us
  transfers between devices with their start and end apart: 18, of which 17 were waited for; matrix products, arithmetic and copies ran while one was open for 1% of the time, Pallas kernels for 0%

commit v1 on v0

v1 whole, which is shorter than its diff:
```python
import jax
import jax.numpy as jnp
from jax import lax
from jax.sharding import PartitionSpec as P

STEPS = 8


def lat_sum(u):
    upper = jnp.pad(u[..., 1:], ((0, 0), (0, 0), (0, 1)))
    lower = jnp.pad(u[..., :-1], ((0, 0), (0, 0), (1, 0)))
    return upper + lower


def loop_pairs(groups, shards, members):
    pieces = groups // members
    pairs = []
    for piece in range(pieces):
        for member in range(members):
            for shard in range(shards):
                here = (piece * members + member) * shards + shard
                if piece + 1 < pieces:
                    there = ((piece + 1) * members + member) * shards + shard
                else:
                    there = member * shards + (shard + 1) % shards
                pairs.append((here, there))
    return pairs


def on_device(field, eof_basis, band_of_mode, coef_table):
    groups, shards = lax.axis_size("lev"), lax.axis_size("lon")
    members, levels, lons, lats = field.shape
    pieces = groups // members
    width = lons // pieces
    cut = field.reshape(members, levels, pieces, width, lats).transpose(2, 0, 1, 3, 4)
    cut = cut.reshape(groups, levels * width, lats)
    whole = lax.all_to_all(cut, "lev", 0, 0, tiled=True).reshape(groups * levels, width, lats)
    modes = jnp.einsum("lk,lxy->xky", eof_basis, whole, preferred_element_type=jnp.float32).astype(jnp.bfloat16)
    onward = loop_pairs(groups, shards, members)
    back = [(b, a) for a, b in onward]
    left = lax.ppermute(modes[width - STEPS :], ("lev", "lon"), onward)
    right = lax.ppermute(modes[:STEPS], ("lev", "lon"), back)
    u = jnp.concatenate([left, modes, right], axis=0).astype(jnp.float32)
    onehot = (band_of_mode[:, None] == jnp.arange(coef_table.shape[0])[None, :]).astype(jnp.float32)
    kappa = jnp.dot(onehot, coef_table, precision=lax.Precision.HIGHEST)
    for step in range(STEPS):
        inner = u[1:-1]
        neighbours = u[2:] + u[:-2] + lat_sum(inner)
        u = inner + kappa * (neighbours - 4.0 * inner)
    diffused = u.astype(jnp.bfloat16)
    total = jnp.einsum("lk,xky->lxy", eof_basis, diffused, preferred_element_type=jnp.float32).astype(jnp.bfloat16)
    total = lax.all_to_all(total.reshape(groups, levels * width, lats), "lev", 0, 0, tiled=True)
    total = total.reshape(pieces, members, levels, width, lats).transpose(1, 2, 0, 3, 4)
    return total.reshape(field.shape)


def solution(mesh):
    return jax.shard_map(
        on_device,
        mesh=mesh,
        in_specs=(P(None, "lev", "lon", None), P(), P(), P()),
        out_specs=P(None, "lev", "lon", None),
        check_vma=False,
    )
```

time: 466 us -> 94.6 us (0.20)
  waiting for transfers between devices: 386 us -> 3.82 us
  blocking collectives: 0 us -> 70.4 us
  starting transfers between devices: 22.4 us -> 4.84 us
  between operations: 13.6 us -> 0.22 us
  local copies, waits for them, and re-layouts: 21.8 us -> 9.17 us
  matrix products: 13.7 us -> 1.22 us
    reduce_scatter x1 -> x0, waiting for transfers between devices: 254 us -> none  [on_device(): lax.psum_scatter(jnp.einsum('lk,mlxy->kmxy', columns, field, preferred_el...]
    all_gather x1 -> x0, waiting for transfers between devices: 124 us -> none  [on_device(): lax.all_gather(diffused, 'lev', axis=0, tiled=True)]
    all_to_all x0 -> x2, blocking collectives: none -> 70.4 us  [the longest x1 38.1 us: on_device(): lax.all_to_all(cut, 'lev', 0, 0, tiled=True)]
    ppermute x16 -> x2, starting transfers between devices: 22.4 us -> 4.84 us  [the longest x1 4.27 us: on_device(): right = lax.ppermute(modes[:STEPS], ('lev', 'lon'), back)]
    dot_general x1 -> x0, local copies, waits for them, and re-layouts: 16.4 us -> none  [on_device(): jnp.einsum('lk,mlxy->kmxy', columns, field, preferred_element_type=jnp.fl...]
    dot_general x3, matrix products: 13.7 us -> 1.22 us  [the longest x1 0.59 us: on_device(): jnp.einsum('lk,xky->lxy', eof_basis, diffused, preferred_element_type=jnp...]
    convert_element_type x17 -> x1, other arithmetic: 7.61 us -> 0.14 us  [on_device(): u = jnp.concatenate([left, modes, right], axis=0).astype(jnp.float32)]
    ppermute x16 -> x2, waiting for transfers between devices: 8.73 us -> 3.82 us  [the longest x1 3.82 us: on_device(): left = lax.ppermute(modes[width - STEPS:], ('lev', 'lon'), onward)]
  transfers between devices with their start and end apart: 18 -> 2, of which waited for: 17 -> 1; matrix products, arithmetic and copies ran while one was open for 1% -> 0% of each run, Pallas kernels for 0% -> 0%
where the time goes in v1:
time: 94.6 us; the launch traced here: 94.4 us
  blocking collectives  70.4 us (74%)
  local copies, waits for them, and re-layouts  9.17 us (10%)
  starting transfers between devices  4.84 us (5%)
  other arithmetic  4.76 us (5%)
  waiting for transfers between devices  3.82 us (4%)
  matrix products  1.22 us (1%)
    all_to_all x1, blocking collectives, on_device(): lax.all_to_all(cut, 'lev', 0, 0, tiled=True)  38.1 us
    all_to_all x1, blocking collectives, on_device(): lax.all_to_all(total.reshape(groups, levels * width, lats), 'lev', 0, 0,...  32.2 us
    add x7, other arithmetic, on_device(): u = inner + kappa * (neighbours - 4.0 * inner)  4.62 us
    ppermute x1, starting transfers between devices, on_device(): right = lax.ppermute(modes[:STEPS], ('lev', 'lon'), back)  4.27 us
    ppermute x1, waiting for transfers between devices, on_device(): left = lax.ppermute(modes[width - STEPS:], ('lev', 'lon'), onward)  3.82 us
    slice x8, local copies, waits for them, and re-layouts, lat_sum(): upper = jnp.pad(u[..., 1:], ((0, 0), (0, 0), (0, 1)))  3.49 us
    unnamed x7, local copies, waits for them, and re-layouts  2.1 us
  transfers between devices with their start and end apart: 2, of which 1 were waited for; matrix products, arithmetic and copies ran while one was open for 0% of the time, Pallas kernels for 0%

profile of v1, /device:TPU:2, one launch (start us, length us, event | category | flops | bytes accessed | tf_op | source)
XLA Modules:
  0.0 94.4 jit_solution(3659661630110580916)
XLA Ops:
  0.0 2.1 %copy.13 = bf16[2,9,96,256]{3,0,2,1:T(2,128)(2,1)S(1)} copy(bf16[2,9,96,256]{3,2,1,0:T(8,128)(2,1)} %param.4) | data formatting | bytes 1769472 | tf_op args[0]
  2.3 0.2 reshape.27
  2.5 38.1 %all_to_all.10 = bf16[16,108,256]{2,1,0:T(8,128)(2,1)S(1)} all-to-all(bf16[16,108,256]{2,1,0:T(8,128)(2,1)S(1)} %reshape.27), channel_id=1, replica_groups=mesh['lev'=16,'lon'=16] {'lev'}, dimensions={0} | all-to-all | bytes 1769472 | tf_op jit(solution)/shard_map/all_to_all | solution.py:37
  40.7 0.2 reshape.22
  40.9 0.4 fusion.17
  41.4 0.6 collective-permute-start
  42.0 4.3 %collective-permute-start.1 = (bf16[8,64,256]{2,1,0:T(8,128)(2,1)S(1)}, bf16[8,64,256]{2,1,0:T(8,128)(2,1)S(1)}, u32[]{:S(2)}, u32[]{:S(2)}) collective-permute-start(bf16[8,64,256]{2,1,0:T(8,128)(2,1)S(1)} %get-tuple-element.22), channel_id=1, source_target_pairs={{32,0},{33,1},{34,2},{35,3},{36,4},{37,5},{38,6},{39,7},{40,8},{41... | collective-permute-start | bytes 786440 | tf_op jit(solution)/shard_map/ppermute | solution.py:42
  46.3 0.2 fusion.41
  46.5 3.8 %collective-permute-done = bf16[8,64,256]{2,1,0:T(8,128)(2,1)S(1)} collective-permute-done((bf16[8,64,256]{2,1,0:T(8,128)(2,1)S(1)}, bf16[8,64,256]{2,1,0:T(8,128)(2,1)S(1)}, u32[]{:S(2)}, u32[]{:S(2)}) %collective-permute-start) | collective-permute-done | bytes 262176 | tf_op jit(solution)/shard_map/ppermute | solution.py:41
  50.4 0.6 fusion.45
  51.1 0.9 fusion.3
  51.9 0.6 fusion.46
  52.5 0.8 fusion.7
  53.3 0.5 fusion.47
  53.8 0.7 fusion.11
  54.6 0.4 fusion.48
  55.0 0.6 fusion.16
  55.6 0.4 fusion.49
  56.0 0.6 fusion.21
  56.6 0.4 fusion.50
  57.0 0.6 fusion.25
  57.6 0.3 fusion.51
  57.9 0.5 fusion.29
  58.4 0.3 fusion.52
  58.7 0.6 fusion.12
  59.3 0.3 copy.17
  59.6 0.2 reshape.23
  59.8 32.2 %all_to_all.11 = bf16[16,108,256]{2,1,0:T(8,128)(2,1)S(1)} all-to-all(bf16[16,108,256]{2,1,0:T(8,128)(2,1)S(1)} %reshape.23), channel_id=1, replica_groups=mesh['lev'=16,'lon'=16] {'lev'}, dimensions={0} | all-to-all | bytes 1769472 | tf_op jit(solution)/shard_map/all_to_all | solution.py:52
  92.1 0.3 copy.18
  92.4 0.3 reshape.24
  92.7 0.7 copy.19
  93.4 1.1 %copy.20 = bf16[2,9,96,256]{3,2,1,0:T(8,128)(2,1)} copy(bf16[2,9,96,256]{3,0,2,1:T(2,128)(2,1)S(1)} %bitcast.18) | data formatting | bytes 1769472 | tf_op jit(solution)/shard_map/reshape | solution.py:54
  (10 shorter events, 0.4 us)
Async XLA Ops:
  0.0 40.9 %copy-start = (bf16[144,64]{0,1:T(8,128)(2,1)S(1)}, bf16[144,64]{0,1:T(8,128)(2,1)}, u32[]{:S(2)}) copy-start(bf16[144,64]{0,1:T(8,128)(2,1)} %param.5) | copy-start | bytes 55300
  40.9 5.3 %copy-start.1 = (f32[8,256]{1,0:T(8,128)S(1)}, f32[8,256]{1,0:T(8,128)}, u32[]{:S(2)}) copy-start(f32[8,256]{1,0:T(8,128)} %param.7) | copy-start | bytes 24580
  40.9 5.3 %copy-start.2 = (s32[64]{0:T(128)S(1)}, s32[64]{0:T(128)}, u32[]{:S(2)}) copy-start(s32[64]{0:T(128)} %param.6) | copy-start | bytes 772
  41.4 8.9 %collective-permute-start = (bf16[8,64,256]{2,1,0:T(8,128)(2,1)S(1)}, bf16[8,64,256]{2,1,0:T(8,128)(2,1)S(1)}, u32[]{:S(2)}, u32[]{:S(2)}) collective-permute-start(bf16[8,64,256]{2,1,0:T(8,128)(2,1)S(1)} %get-tuple-element.21), channel_id=1, source_target_pairs={{0,32},{1,33},{2,34},{3,35},{4,36},{5,37},{6,38},{7,39},{8,40},{9,... | collective-permute-start | bytes 786440 | tf_op jit(solution)/shard_map/ppermute | solution.py:41
  42.0 8.3 %collective-permute-start.1 = (bf16[8,64,256]{2,1,0:T(8,128)(2,1)S(1)}, bf16[8,64,256]{2,1,0:T(8,128)(2,1)S(1)}, u32[]{:S(2)}, u32[]{:S(2)}) collective-permute-start(bf16[8,64,256]{2,1,0:T(8,128)(2,1)S(1)} %get-tuple-element.22), channel_id=1, source_target_pairs={{32,0},{33,1},{34,2},{35,3},{36,4},{37,5},{38,6},{39,7},{40,8},{41... | collective-permute-start | bytes 786440 | tf_op jit(solution)/shard_map/ppermute | solution.py:42

commit v2 on v1

v2 whole, which is shorter than its diff:
```python
import functools

import jax
import jax.numpy as jnp
from jax import lax
from jax.experimental import pallas as pl
from jax.experimental.pallas import tpu as pltpu
from jax.sharding import PartitionSpec as P

STEPS = 8
ROWS = 16
SPLITS = 1
LANES = 128


def place(piece, shard, pieces):
    return piece + (shard % 2) * (pieces - 1 - 2 * piece)


def loop_pairs(groups, shards, members):
    pieces = groups // members
    pairs = []
    for shard in range(shards):
        for piece in range(pieces):
            for member in range(members):
                carry, after = divmod(piece + 1, pieces)
                then = (shard + carry) % shards
                here = place(piece, shard, pieces) * members + member
                there = place(after, then, pieces) * members + member
                pairs.append((here * shards + shard, there * shards + then))
    return pairs


def pack_kernel(pieces, field_ref, out_ref, held_ref, sems):
    members, levels, lons, lats = field_ref.shape
    width = lons // pieces
    shard = lax.axis_index("lon")
    copies = []
    for level in range(levels):
        for member in range(members):
            copy = pltpu.make_async_copy(field_ref.at[member, level], held_ref.at[member, level], sems.at[member, level])
            copy.start()
            copies.append(copy)
    for level in range(levels):
        for member in range(members):
            copies[level * members + member].wait()
            for piece in range(pieces):
                to = place(piece, shard, pieces) * members + member
                out_ref[to, level * width : (level + 1) * width, :] = held_ref[
                    member, level, piece * width : (piece + 1) * width, :
                ]


def pack(field, pieces):
    members, levels, lons, lats = field.shape
    return pl.pallas_call(
        functools.partial(pack_kernel, pieces),
        out_shape=jax.ShapeDtypeStruct((pieces * members, levels * (lons // pieces), lats), field.dtype),
        in_specs=[pl.BlockSpec(memory_space=pl.ANY)],
        out_specs=pl.BlockSpec(memory_space=pltpu.VMEM),
        scratch_shapes=[pltpu.VMEM(field.shape, field.dtype), pltpu.SemaphoreType.DMA((members, levels))],
        compiler_params=pltpu.CompilerParams(vmem_limit_bytes=16 * 1024 * 1024),
        name="pack",
    )(field)


def unpack_kernel(pieces, blocks_ref, out_ref, held_ref, sems):
    members, levels, lons, lats = out_ref.shape
    width = lons // pieces
    shard = lax.axis_index("lon")
    copies = []
    for level in range(levels):
        for member in range(members):
            for piece in range(pieces):
                at = place(piece, shard, pieces) * members + member
                held_ref[member, level, piece * width : (piece + 1) * width, :] = blocks_ref[
                    at, level * width : (level + 1) * width, :
                ]
            copy = pltpu.make_async_copy(held_ref.at[member, level], out_ref.at[member, level], sems.at[member, level])
            copy.start()
            copies.append(copy)
    for copy in copies:
        copy.wait()


def unpack(blocks, shape, pieces):
    members, levels, lons, lats = shape
    return pl.pallas_call(
        functools.partial(unpack_kernel, pieces),
        out_shape=jax.ShapeDtypeStruct(shape, blocks.dtype),
        in_specs=[pl.BlockSpec(memory_space=pltpu.VMEM)],
        out_specs=pl.BlockSpec(memory_space=pl.ANY),
        scratch_shapes=[pltpu.VMEM(shape, blocks.dtype), pltpu.SemaphoreType.DMA((members, levels))],
        compiler_params=pltpu.CompilerParams(vmem_limit_bytes=16 * 1024 * 1024),
        name="unpack",
    )(blocks)


def lat_sum(halves, first, last):
    ups = [pltpu.roll(half, 1, 1) for half in halves]
    downs = [pltpu.roll(half, LANES - 1, 1) for half in halves]
    out = []
    for i in range(len(halves)):
        below = ups[i - 1] if i else 0.0
        above = downs[i + 1] if i + 1 < len(halves) else 0.0
        out.append(jnp.where(first, below, ups[i]) + jnp.where(last, above, downs[i]))
    return out


def diffuse(modes_ref, left_ref, right_ref, kappa_ref, out_ref, u_ref):
    width, count, lats = modes_ref.shape
    tiles = lats // LANES
    lane = lax.broadcasted_iota(jnp.int32, (ROWS, LANES), 1)
    first, last = lane == 0, lane == LANES - 1

    def cut(x):
        return [x[:, i * LANES : (i + 1) * LANES] for i in range(tiles)]

    def block(index, carry):
        rows = pl.ds(pl.multiple_of(index * ROWS, ROWS), ROWS)
        kappa = cut(kappa_ref[rows, :])
        keep = [1.0 - 4.0 * k for k in kappa]
        total = width + 2 * STEPS

        def start(column):
            if column < STEPS:
                ref, at = left_ref, column
            elif column < STEPS + width:
                ref, at = modes_ref, column - STEPS
            else:
                ref, at = right_ref, column - STEPS - width
            return cut(ref[at, rows, :].astype(jnp.float32))

        for step in range(STEPS):
            get = start if step == 0 else (lambda column: cut(u_ref[column]))
            before, here = get(step), get(step + 1)
            for column in range(step + 1, total - step - 1):
                after = get(column + 1)
                sides = lat_sum(here, first, last)
                new = [
                    c * h + k * ((b + a) + s)
                    for c, h, k, b, a, s in zip(keep, here, kappa, before, after, sides)
                ]
                new = jnp.concatenate(new, axis=1)
                if step + 1 < STEPS:
                    u_ref[column] = new
                else:
                    out_ref[column - STEPS, rows, :] = new.astype(out_ref.dtype)
                before, here = here, after
        return carry

    lax.fori_loop(0, count // ROWS, block, 0)


def diffused(modes, left, right, kappa):
    width, count, lats = modes.shape
    return pl.pallas_call(
        diffuse,
        out_shape=jax.ShapeDtypeStruct(modes.shape, jnp.bfloat16),
        in_specs=[pl.BlockSpec(memory_space=pltpu.VMEM)] * 4,
        out_specs=pl.BlockSpec(memory_space=pltpu.VMEM),
        scratch_shapes=[pltpu.VMEM((width + 2 * STEPS, ROWS, lats), jnp.float32)],
        compiler_params=pltpu.CompilerParams(vmem_limit_bytes=16 * 1024 * 1024),
        cost_estimate=pl.CostEstimate(flops=60 * count * lats * (width + STEPS), bytes_accessed=6 * count * lats * width, transcendentals=0),
        name="diffuse",
    )(modes, left, right, kappa)


def on_device(field, eof_basis, band_of_mode, coef_table):
    groups, shards = lax.axis_size("lev"), lax.axis_size("lon")
    members, levels, lons, lats = field.shape
    pieces = groups // members
    width = lons // pieces
    count = eof_basis.shape[1]
    cut = pack(field, pieces)
    whole = lax.all_to_all(cut, "lev", 0, 0, tiled=True).reshape(groups * levels, width, lats)
    modes = jnp.einsum("lk,lxy->xky", eof_basis, whole, preferred_element_type=jnp.float32).astype(jnp.bfloat16)
    onward = loop_pairs(groups, shards, members)
    back = [(b, a) for a, b in onward]
    onehot = (band_of_mode[:, None] == jnp.arange(coef_table.shape[0])[None, :]).astype(jnp.float32)
    kappa = jnp.dot(onehot, coef_table, precision=lax.Precision.HIGHEST)
    share = count // SPLITS
    parts = []
    for split in range(SPLITS):
        some = modes[:, split * share : (split + 1) * share]
        left = lax.ppermute(some[width - STEPS :], ("lev", "lon"), onward)
        right = lax.ppermute(some[:STEPS], ("lev", "lon"), back)
        parts.append(diffused(some, left, right, kappa[split * share : (split + 1) * share]))
    final = jnp.concatenate(parts, axis=1) if SPLITS > 1 else parts[0]
    total = jnp.einsum("lk,xky->lxy", eof_basis, final, preferred_element_type=jnp.float32).astype(jnp.bfloat16)
    total = lax.all_to_all(total.reshape(groups, levels * width, lats), "lev", 0, 0, tiled=True)
    return unpack(total, field.shape, pieces)


def solution(mesh):
    return jax.shard_map(
        on_device,
        mesh=mesh,
        in_specs=(P(None, "lev", "lon", None), P(), P(), P()),
        out_specs=P(None, "lev", "lon", None),
        check_vma=False,
    )
```

time: 94.6 us -> 89.9 us (0.950)
  Pallas kernels: 0 us -> 7.52 us
  local copies, waits for them, and re-layouts: 9.17 us -> 2.01 us
  other arithmetic: 4.76 us -> 0 us
  starting transfers between devices: 4.84 us -> 2.73 us
  blocking collectives: 70.4 us -> 72.4 us
    pallas_call x0 -> x3, Pallas kernels: none -> 7.52 us  [the longest x1 5 us: diffused(): pl.pallas_call(diffuse, out_shape=jax.ShapeDtypeStruct(modes.shape, jnp.b...]
    add x7 -> x0, other arithmetic: 4.62 us -> none  [on_device(): u = inner + kappa * (neighbours - 4.0 * inner)]
    slice x9 -> x1, local copies, waits for them, and re-layouts: 3.53 us -> 0.04 us  [on_device(): right = lax.ppermute(some[:STEPS], ('lev', 'lon'), back)]
    ppermute x2, starting transfers between devices: 4.84 us -> 2.73 us  [the longest x1 2.16 us: on_device(): right = lax.ppermute(some[:STEPS], ('lev', 'lon'), back)]
    all_to_all x1, blocking collectives: 32.2 us -> 34.2 us  [on_device(): lax.all_to_all(total.reshape(groups, levels * width, lats), 'lev', 0, 0,...]
    reshape x4 -> x0, local copies, waits for them, and re-layouts: 1.82 us -> none  [the longest x1 1.06 us: on_device(): return total.reshape(field.shape)]
    unnamed x7 -> x8, local copies, waits for them, and re-layouts: 2.1 us -> 1.19 us
  transfers between devices with their start and end apart: 2 -> 2, of which waited for: 1 -> 2; matrix products, arithmetic and copies ran while one was open for 0% -> 0% of each run, Pallas kernels for 0% -> 0%
where the time goes in v2:
time: 89.9 us; the launch traced here: 89.8 us
  blocking collectives  72.4 us (81%)
  Pallas kernels  7.52 us (8%)
  waiting for transfers between devices  3.98 us (4%)
  starting transfers between devices  2.73 us (3%)
  local copies, waits for them, and re-layouts  2.01 us (2%)
  matrix products  1.06 us (1%)
    all_to_all x1, blocking collectives, on_device(): lax.all_to_all(cut, 'lev', 0, 0, tiled=True)  38.1 us
    all_to_all x1, blocking collectives, on_device(): lax.all_to_all(total.reshape(groups, levels * width, lats), 'lev', 0, 0,...  34.2 us
    pallas_call x1, Pallas kernels, diffused(): pl.pallas_call(diffuse, out_shape=jax.ShapeDtypeStruct(modes.shape, jnp.b...  5 us
    ppermute x1, waiting for transfers between devices, on_device(): left = lax.ppermute(some[width - STEPS:], ('lev', 'lon'), onward)  3.93 us
    ppermute x1, starting transfers between devices, on_device(): right = lax.ppermute(some[:STEPS], ('lev', 'lon'), back)  2.16 us
  transfers between devices with their start and end apart: 2, of which 2 were waited for; matrix products, arithmetic and copies ran while one was open for 0% of the time, Pallas kernels for 0%

profile of v2, /device:TPU:2, one launch (start us, length us, event | category | flops | bytes accessed | tf_op | source)
XLA Modules:
  0.0 89.8 jit_solution(12033446556681481885)
XLA Ops:
  0.0 0.0 copy-start
  0.0 0.0 copy-start.1
  0.0 1.2 %copy-done.1 = bf16[2,9,96,256]{3,2,1,0:T(8,128)(2,1)S(1)} copy-done((bf16[2,9,96,256]{3,2,1,0:T(8,128)(2,1)S(1)}, bf16[2,9,96,256]{3,2,1,0:T(8,128)(2,1)}, u32[]{:S(2)}) %copy-start.1) | copy-done | bytes 884760
  1.2 1.5 %pack.1 = bf16[16,108,256]{2,1,0:T(8,128)(2,1)S(1)} custom-call(bf16[2,9,96,256]{3,2,1,0:T(8,128)(2,1)S(1)} %copy-done.1), custom_call_target="tpu_custom_call" | custom-call | tf_op jit(solution)/shard_map/pack/pallas_call | solution.py:56
  2.7 38.1 %all_to_all.10 = bf16[16,108,256]{2,1,0:T(8,128)(2,1)S(1)} all-to-all(bf16[16,108,256]{2,1,0:T(8,128)(2,1)S(1)} %pack.1), channel_id=1, replica_groups=mesh['lev'=16,'lon'=16] {'lev'}, dimensions={0} | all-to-all | bytes 1769472 | tf_op jit(solution)/shard_map/all_to_all | solution.py:176
  40.8 0.2 reshape.7
  41.0 0.0 copy-done
  41.0 0.0 copy-start.2
  41.0 0.0 copy-start.3
  41.1 0.4 fusion.1.modes_ref
  41.5 0.6 collective-permute-start
  42.1 2.2 %collective-permute-start.1 = (bf16[8,64,256]{2,1,0:T(8,128)(2,1)S(1)}, bf16[8,64,256]{2,1,0:T(8,128)(2,1)S(1)}, u32[]{:S(2)}, u32[]{:S(2)}) collective-permute-start(bf16[8,64,256]{2,1,0:T(8,128)(2,1)S(1)} %get-tuple-element.5), channel_id=1, source_target_pairs={{32,0},{48,16},{64,32},{80,48},{96,64},{112,80},{128,96},{144,112}... | collective-permute-start | bytes 786440 | tf_op jit(solution)/shard_map/ppermute | solution.py:187
  44.3 0.0 copy-done.2
  44.3 0.0 copy-done.3
  44.3 0.2 fusion.5.kappa_ref
  44.5 3.9 %collective-permute-done.left_ref = bf16[8,64,256]{2,1,0:T(8,128)(2,1)S(1)} collective-permute-done((bf16[8,64,256]{2,1,0:T(8,128)(2,1)S(1)}, bf16[8,64,256]{2,1,0:T(8,128)(2,1)S(1)}, u32[]{:S(2)}, u32[]{:S(2)}) %collective-permute-start) | collective-permute-done | bytes 262176 | tf_op jit(solution)/shard_map/ppermute | solution.py:186
  48.4 0.1 collective-permute-done.1.right_ref
  48.5 5.0 %diffuse.1 = bf16[12,64,256]{2,1,0:T(8,128)(2,1)S(1)} custom-call(bf16[12,64,256]{2,1,0:T(8,128)(2,1)S(1)} %fusion.1.modes_ref, bf16[8,64,256]{2,1,0:T(8,128)(2,1)S(1)} %collective-permute-done.left_ref, bf16[8,64,256]{2,1,0:T(8,128)(2,1)S(1)} %collective-permute-done.1.right_ref, f32[64,256]{1,0:T(8,128)S(1)} %fusion.5.kappa_ref), custom_call_target="tpu_custom_call" | custom-call | flops 19660800 | bytes 1179648 | tf_op jit(solution)/shard_map/diffuse/pallas_call | solution.py:157
  53.5 0.4 fusion
  53.9 0.3 copy.8
  54.3 0.2 reshape.8
  54.5 34.2 %all_to_all.11.blocks_ref = bf16[16,108,256]{2,1,0:T(8,128)(2,1)S(1)} all-to-all(bf16[16,108,256]{2,1,0:T(8,128)(2,1)S(1)} %reshape.8), channel_id=1, replica_groups=mesh['lev'=16,'lon'=16] {'lev'}, dimensions={0} | all-to-all | bytes 1769472 | tf_op jit(solution)/shard_map/all_to_all | solution.py:191
  88.7 1.1 %unpack.1 = bf16[2,9,96,256]{3,2,1,0:T(8,128)(2,1)} custom-call(bf16[16,108,256]{2,1,0:T(8,128)(2,1)S(1)} %all_to_all.11.blocks_ref), custom_call_target="tpu_custom_call" | custom-call | tf_op jit(solution)/shard_map/unpack/pallas_call | solution.py:88
  (1 shorter events, 0.0 us)
Async XLA Ops:
  0.0 41.0 %copy-start = (bf16[144,64]{0,1:T(8,128)(2,1)S(1)}, bf16[144,64]{0,1:T(8,128)(2,1)}, u32[]{:S(2)}) copy-start(bf16[144,64]{0,1:T(8,128)(2,1)} %param.5) | copy-start | bytes 55300
  0.0 1.2 %copy-start.1 = (bf16[2,9,96,256]{3,2,1,0:T(8,128)(2,1)S(1)}, bf16[2,9,96,256]{3,2,1,0:T(8,128)(2,1)}, u32[]{:S(2)}) copy-start(bf16[2,9,96,256]{3,2,1,0:T(8,128)(2,1)} %field_ref.1) | copy-start | bytes 2654212
  41.0 3.2 %copy-start.2 = (f32[8,256]{1,0:T(8,128)S(1)}, f32[8,256]{1,0:T(8,128)}, u32[]{:S(2)}) copy-start(f32[8,256]{1,0:T(8,128)} %param.7) | copy-start | bytes 24580
  41.0 3.2 %copy-start.3 = (s32[64]{0:T(128)S(1)}, s32[64]{0:T(128)}, u32[]{:S(2)}) copy-start(s32[64]{0:T(128)} %param.6) | copy-start | bytes 772
  41.5 6.9 %collective-permute-start = (bf16[8,64,256]{2,1,0:T(8,128)(2,1)S(1)}, bf16[8,64,256]{2,1,0:T(8,128)(2,1)S(1)}, u32[]{:S(2)}, u32[]{:S(2)}) collective-permute-start(bf16[8,64,256]{2,1,0:T(8,128)(2,1)S(1)} %get-tuple-element.6), channel_id=1, source_target_pairs={{0,32},{16,48},{32,64},{48,80},{64,96},{80,112},{96,128},{112,144}... | collective-permute-start | bytes 786440 | tf_op jit(solution)/shard_map/ppermute | solution.py:186
  42.1 6.4 %collective-permute-start.1 = (bf16[8,64,256]{2,1,0:T(8,128)(2,1)S(1)}, bf16[8,64,256]{2,1,0:T(8,128)(2,1)S(1)}, u32[]{:S(2)}, u32[]{:S(2)}) collective-permute-start(bf16[8,64,256]{2,1,0:T(8,128)(2,1)S(1)} %get-tuple-element.5), channel_id=1, source_target_pairs={{32,0},{48,16},{64,32},{80,48},{96,64},{112,80},{128,96},{144,112}... | collective-permute-start | bytes 786440 | tf_op jit(solution)/shard_map/ppermute | solution.py:187

commit v3 on v2

--- a/solution.py
+++ b/solution.py
@@ -9,7 +9,7 @@
 
 STEPS = 8
 ROWS = 16
-SPLITS = 1
+SPLITS = 2
 LANES = 128
 
 
@@ -31,22 +31,39 @@
     return pairs
 
 
-def pack_kernel(pieces, field_ref, out_ref, held_ref, sems):
+def sending_order(pieces):
+    return list(range(0, pieces, 2)) + list(range(1, pieces, 2))
+
+
+def slot(member, piece, pieces):
+    return member * pieces + sending_order(pieces).index(piece)
+
+
+def owners(shard, pieces, members):
+    return [place(piece, shard, pieces) * members + member for member in range(members) for piece in sending_order(pieces)]
+
+
+def exchange(blocks, groups, shards, members):
+    order = [[lev * shards + shard for lev in owners(shard, groups // members, members)] for shard in range(shards)]
+    return lax.all_to_all(blocks, ("lev", "lon"), 0, 0, tiled=True, axis_index_groups=order)
+
+
+def basis_by_owner(basis, groups, members):
+    rows = basis.shape[0] // groups
+
+    def ordered(shard):
+        return jnp.concatenate([basis[lev * rows : (lev + 1) * rows] for lev in owners(shard, groups // members, members)])
+
+    return jnp.where(lax.axis_index("lon") % 2 == 0, ordered(0), ordered(1))
+
+
+def pack_kernel(pieces, field_ref, out_ref):
     members, levels, lons, lats = field_ref.shape
     width = lons // pieces
-    shard = lax.axis_index("lon")
-    copies = []
     for level in range(levels):
         for member in range(members):
-            copy = pltpu.make_async_copy(field_ref.at[member, level], held_ref.at[member, level], sems.at[member, level])
-            copy.start()
-            copies.append(copy)
-    for level in range(levels):
-        for member in range(members):
-            copies[level * members + member].wait()
             for piece in range(pieces):
-                to = place(piece, shard, pieces) * members + member
-                out_ref[to, level * width : (level + 1) * width, :] = held_ref[
+                out_ref[slot(member, piece, pieces), level * width : (level + 1) * width, :] = field_ref[
                     member, level, piece * width : (piece + 1) * width, :
                 ]
 
@@ -56,9 +73,8 @@
     return pl.pallas_call(
         functools.partial(pack_kernel, pieces),
         out_shape=jax.ShapeDtypeStruct((pieces * members, levels * (lons // pieces), lats), field.dtype),
-        in_specs=[pl.BlockSpec(memory_space=pl.ANY)],
+        in_specs=[pl.BlockSpec(memory_space=pltpu.VMEM)],
         out_specs=pl.BlockSpec(memory_space=pltpu.VMEM),
-        scratch_shapes=[pltpu.VMEM(field.shape, field.dtype), pltpu.SemaphoreType.DMA((members, levels))],
         compiler_params=pltpu.CompilerParams(vmem_limit_bytes=16 * 1024 * 1024),
         name="pack",
     )(field)
@@ -67,14 +83,12 @@
 def unpack_kernel(pieces, blocks_ref, out_ref, held_ref, sems):
     members, levels, lons, lats = out_ref.shape
     width = lons // pieces
-    shard = lax.axis_index("lon")
     copies = []
     for level in range(levels):
         for member in range(members):
             for piece in range(pieces):
-                at = place(piece, shard, pieces) * members + member
                 held_ref[member, level, piece * width : (piece + 1) * width, :] = blocks_ref[
-                    at, level * width : (level + 1) * width, :
+                    slot(member, piece, pieces), level * width : (level + 1) * width, :
                 ]
             copy = pltpu.make_async_copy(held_ref.at[member, level], out_ref.at[member, level], sems.at[member, level])
             copy.start()
@@ -172,9 +186,10 @@
     pieces = groups // members
     width = lons // pieces
     count = eof_basis.shape[1]
+    basis = basis_by_owner(eof_basis, groups, members)
     cut = pack(field, pieces)
-    whole = lax.all_to_all(cut, "lev", 0, 0, tiled=True).reshape(groups * levels, width, lats)
-    modes = jnp.einsum("lk,lxy->xky", eof_basis, whole, preferred_element_type=jnp.float32).astype(jnp.bfloat16)
+    whole = exchange(cut, groups, shards, members).reshape(groups * levels, width, lats)
+    modes = jnp.einsum("lk,lxy->xky", basis, whole, preferred_element_type=jnp.float32).astype(jnp.bfloat16)
     onward = loop_pairs(groups, shards, members)
     back = [(b, a) for a, b in onward]
     onehot = (band_of_mode[:, None] == jnp.arange(coef_table.shape[0])[None, :]).astype(jnp.float32)
@@ -187,8 +202,8 @@
         right = lax.ppermute(some[:STEPS], ("lev", "lon"), back)
         parts.append(diffused(some, left, right, kappa[split * share : (split + 1) * share]))
     final = jnp.concatenate(parts, axis=1) if SPLITS > 1 else parts[0]
-    total = jnp.einsum("lk,xky->lxy", eof_basis, final, preferred_element_type=jnp.float32).astype(jnp.bfloat16)
-    total = lax.all_to_all(total.reshape(groups, levels * width, lats), "lev", 0, 0, tiled=True)
+    total = jnp.einsum("lk,xky->lxy", basis, final, preferred_element_type=jnp.float32).astype(jnp.bfloat16)
+    total = exchange(total.reshape(groups, levels * width, lats), groups, shards, members)
     return unpack(total, field.shape, pieces)
 
 

time: 89.9 us -> 82.4 us (0.917)
  blocking collectives: 72.4 us -> 30.3 us
  waiting for transfers between devices: 3.98 us -> 24.3 us
  starting transfers between devices: 2.73 us -> 16.7 us
    all_to_all x2 -> x1, blocking collectives: 72.4 us -> 30.3 us  [exchange(): lax.all_to_all(blocks, ('lev', 'lon'), 0, 0, tiled=True, axis_index_group...]
    all_to_all x0 -> x1, waiting for transfers between devices: none -> 23 us  [exchange(): lax.all_to_all(blocks, ('lev', 'lon'), 0, 0, tiled=True, axis_index_group...]
    all_to_all x0 -> x1, starting transfers between devices: none -> 11.3 us  [exchange(): lax.all_to_all(blocks, ('lev', 'lon'), 0, 0, tiled=True, axis_index_group...]
    ppermute x1 -> x2, waiting for transfers between devices: 3.93 us -> 0.08 us  [on_device(): left = lax.ppermute(some[width - STEPS:], ('lev', 'lon'), onward)]
    ppermute x1 -> x2, starting transfers between devices: 2.16 us -> 5.07 us  [on_device(): right = lax.ppermute(some[:STEPS], ('lev', 'lon'), back)]
    ppermute x1 -> x2, waiting for transfers between devices: 0.05 us -> 1.22 us  [on_device(): right = lax.ppermute(some[:STEPS], ('lev', 'lon'), back)]
    pallas_call x1 -> x2, Pallas kernels: 5 us -> 5.01 us  [diffused(): pl.pallas_call(diffuse, out_shape=jax.ShapeDtypeStruct(modes.shape, jnp.b...]
  transfers between devices with their start and end apart: 2 -> 5, of which waited for: 2 -> 3; matrix products, arithmetic and copies ran while one was open for 0% -> 1% of each run, Pallas kernels for 0% -> 3%
where the time goes in v3:
time: 82.4 us; the launch traced here: 82.1 us
  blocking collectives  30.3 us (37%)
  waiting for transfers between devices  24.3 us (29%)
  starting transfers between devices  16.7 us (20%)
  Pallas kernels  7.09 us (9%)
  local copies, waits for them, and re-layouts  2.47 us (3%)
  matrix products  1.04 us (1%)
    all_to_all x1, blocking collectives, exchange(): lax.all_to_all(blocks, ('lev', 'lon'), 0, 0, tiled=True, axis_index_group...  30.3 us
    all_to_all x1, waiting for transfers between devices, exchange(): lax.all_to_all(blocks, ('lev', 'lon'), 0, 0, tiled=True, axis_index_group...  23 us
    all_to_all x1, starting transfers between devices, exchange(): lax.all_to_all(blocks, ('lev', 'lon'), 0, 0, tiled=True, axis_index_group...  11.3 us
    ppermute x2, starting transfers between devices, on_device(): right = lax.ppermute(some[:STEPS], ('lev', 'lon'), back)  5.07 us
    pallas_call x2, Pallas kernels, diffused(): pl.pallas_call(diffuse, out_shape=jax.ShapeDtypeStruct(modes.shape, jnp.b...  5.01 us
  transfers between devices with their start and end apart: 5, of which 3 were waited for; matrix products, arithmetic and copies ran while one was open for 1% of the time, Pallas kernels for 3%

profile of v3, /device:TPU:2, one launch (start us, length us, event | category | flops | bytes accessed | tf_op | source)
XLA Modules:
  0.0 82.1 jit_solution(8376013254838554062)
XLA Ops:
  0.0 0.0 copy-start
  0.0 0.0 copy-start.1
  0.0 1.2 %copy-done.1 = bf16[2,9,96,256]{3,2,1,0:T(8,128)(2,1)S(1)} copy-done((bf16[2,9,96,256]{3,2,1,0:T(8,128)(2,1)S(1)}, bf16[2,9,96,256]{3,2,1,0:T(8,128)(2,1)}, u32[]{:S(2)}) %copy-start.1) | copy-done | bytes 884760
  1.2 1.0 %pack.1 = bf16[16,108,256]{2,1,0:T(8,128)(2,1)} custom-call(bf16[2,9,96,256]{3,2,1,0:T(8,128)(2,1)S(1)} %copy-done.1), custom_call_target="tpu_custom_call" | custom-call | tf_op jit(solution)/shard_map/pack/pallas_call | solution.py:73
  2.2 0.0 copy-start.2
  2.2 0.0 copy-start.3
  2.2 11.3 %all-to-all-start = ((bf16[16,108,256]{2,1,0:T(8,128)(2,1)}), bf16[16,108,256]{2,1,0:T(8,128)(2,1)S(1)}, u32[]{:S(2)}, u32[]{:S(2)}) async-start(bf16[16,108,256]{2,1,0:T(8,128)(2,1)} %pack.1), calls=%async_computation | async-start | bytes 1835008 | tf_op jit(solution)/shard_map/all_to_all | solution.py:48
  13.6 0.0 copy-done.2
  13.6 0.1 fusion.13
  13.7 0.2 concatenate.9
  13.9 0.2 concatenate.10
  14.0 0.0 copy-done
  14.1 0.0 copy-done.3
  14.1 0.2 fusion.7
  14.3 23.0 %all-to-all-done = bf16[16,108,256]{2,1,0:T(8,128)(2,1)S(1)} async-done(((bf16[16,108,256]{2,1,0:T(8,128)(2,1)}), bf16[16,108,256]{2,1,0:T(8,128)(2,1)S(1)}, u32[]{:S(2)}, u32[]{:S(2)}) %all-to-all-start) | async-done | bytes 884768 | tf_op jit(solution)/shard_map/all_to_all | solution.py:48
  37.3 0.2 reshape.7
  37.5 0.4 fusion
  38.0 0.3 collective-permute-start.2
  38.3 2.4 %collective-permute-start.3 = (bf16[8,32,256]{2,1,0:T(8,128)(2,1)S(1)}, bf16[8,32,256]{2,1,0:T(8,128)(2,1)S(1)}, u32[]{:S(2)}, u32[]{:S(2)}) collective-permute-start(bf16[8,32,256]{2,1,0:T(8,128)(2,1)S(1)} %get-tuple-element.6), channel_id=1, source_target_pairs={{32,0},{48,16},{64,32},{80,48},{96,64},{112,80},{128,96},{144,112}... | collective-permute-start | bytes 393224 | tf_op jit(solution)/shard_map/ppermute | solution.py:202
  40.7 0.0 collective-permute-start
  40.7 2.6 %collective-permute-start.1 = (bf16[8,32,256]{2,1,0:T(8,128)(2,1)S(1)}, bf16[8,32,256]{2,1,0:T(8,128)(2,1)S(1)}, u32[]{:S(2)}, u32[]{:S(2)}) collective-permute-start(bf16[8,32,256]{2,1,0:T(8,128)(2,1)S(1)} %get-tuple-element.5), channel_id=1, source_target_pairs={{32,0},{48,16},{64,32},{80,48},{96,64},{112,80},{128,96},{144,112}... | collective-permute-start | bytes 393224 | tf_op jit(solution)/shard_map/ppermute | solution.py:202
  43.4 0.1 collective-permute-done.2.left_ref
  43.5 1.2 %collective-permute-done.3.right_ref = bf16[8,32,256]{2,1,0:T(8,128)(2,1)S(1)} collective-permute-done((bf16[8,32,256]{2,1,0:T(8,128)(2,1)S(1)}, bf16[8,32,256]{2,1,0:T(8,128)(2,1)S(1)}, u32[]{:S(2)}, u32[]{:S(2)}) %collective-permute-start.3) | collective-permute-done | bytes 131104 | tf_op jit(solution)/shard_map/ppermute | solution.py:202
  44.7 2.5 %diffuse.3 = bf16[12,32,256]{2,1,0:T(8,128)(2,1)S(1)} custom-call(bf16[12,32,256]{2,1,0:T(8,128)(2,1)S(1)} %get-tuple-element.10.modes_ref, bf16[8,32,256]{2,1,0:T(8,128)(2,1)S(1)} %collective-permute-done.2.left_ref, bf16[8,32,256]{2,1,0:T(8,128)(2,1)S(1)} %collective-permute-done.3.right_ref, f32[32,256]{1,0:T(8,128)S(1)} %get-tuple-element.12.kappa_ref), custom_call_target="tpu_custom_call" | custom-call | flops 9830400 | bytes 589824 | tf_op jit(solution)/shard_map/diffuse/pallas_call | solution.py:171
  47.2 0.0 collective-permute-done.left_ref
  47.2 0.0 collective-permute-done.1.right_ref
  47.2 2.5 %diffuse.2 = bf16[12,32,256]{2,1,0:T(8,128)(2,1)S(1)} custom-call(bf16[12,32,256]{2,1,0:T(8,128)(2,1)S(1)} %get-tuple-element.9.modes_ref, bf16[8,32,256]{2,1,0:T(8,128)(2,1)S(1)} %collective-permute-done.left_ref, bf16[8,32,256]{2,1,0:T(8,128)(2,1)S(1)} %collective-permute-done.1.right_ref, f32[32,256]{1,0:T(8,128)S(1)} %get-tuple-element.11.kappa_ref), custom_call_target="tpu_custom_call" | custom-call | flops 9830400 | bytes 589824 | tf_op jit(solution)/shard_map/diffuse/pallas_call | solution.py:171
  49.7 0.4 convolution_convert_fusion
  50.2 0.3 copy.8
  50.5 0.2 reshape.8
  50.7 30.3 %all_to_all.10.blocks_ref = bf16[16,108,256]{2,1,0:T(8,128)(2,1)S(1)} all-to-all(bf16[16,108,256]{2,1,0:T(8,128)(2,1)S(1)} %reshape.8), channel_id=1, replica_groups={{0,64,128,192,32,96,160,224,16,80,144,208,48,112,176,240},{225,161,97,3..., dimensions={0} | all-to-all | bytes 1769472 | tf_op jit(solution)/shard_map/all_to_all | solution.py:48
  81.0 1.1 %unpack.1 = bf16[2,9,96,256]{3,2,1,0:T(8,128)(2,1)} custom-call(bf16[16,108,256]{2,1,0:T(8,128)(2,1)S(1)} %all_to_all.10.blocks_ref), custom_call_target="tpu_custom_call" | custom-call | tf_op jit(solution)/shard_map/unpack/pallas_call | solution.py:102
  (3 shorter events, 0.1 us)
Async XLA Ops:
  0.0 14.0 %copy-start = (f32[8,256]{1,0:T(8,128)S(1)}, f32[8,256]{1,0:T(8,128)}, u32[]{:S(2)}) copy-start(f32[8,256]{1,0:T(8,128)} %param.7) | copy-start | bytes 24580
  0.0 1.2 %copy-start.1 = (bf16[2,9,96,256]{3,2,1,0:T(8,128)(2,1)S(1)}, bf16[2,9,96,256]{3,2,1,0:T(8,128)(2,1)}, u32[]{:S(2)}) copy-start(bf16[2,9,96,256]{3,2,1,0:T(8,128)(2,1)} %field_ref.1) | copy-start | bytes 2654212
  2.2 11.3 %copy-start.2 = (bf16[144,64]{0,1:T(8,128)(2,1)S(1)}, bf16[144,64]{0,1:T(8,128)(2,1)}, u32[]{:S(2)}) copy-start(bf16[144,64]{0,1:T(8,128)(2,1)} %param.5) | copy-start | bytes 55300
  2.2 11.8 %copy-start.3 = (s32[64]{0:T(128)S(1)}, s32[64]{0:T(128)}, u32[]{:S(2)}) copy-start(s32[64]{0:T(128)} %param.6) | copy-start | bytes 772
  2.2 35.1 %all-to-all-start = ((bf16[16,108,256]{2,1,0:T(8,128)(2,1)}), bf16[16,108,256]{2,1,0:T(8,128)(2,1)S(1)}, u32[]{:S(2)}, u32[]{:S(2)}) async-start(bf16[16,108,256]{2,1,0:T(8,128)(2,1)} %pack.1), calls=%async_computation | async-start | bytes 1835008 | tf_op jit(solution)/shard_map/all_to_all | solution.py:48
  38.0 5.5 %collective-permute-start.2 = (bf16[8,32,256]{2,1,0:T(8,128)(2,1)S(1)}, bf16[8,32,256]{2,1,0:T(8,128)(2,1)S(1)}, u32[]{:S(2)}, u32[]{:S(2)}) collective-permute-start(bf16[8,32,256]{2,1,0:T(8,128)(2,1)S(1)} %get-tuple-element.7), channel_id=1, source_target_pairs={{0,32},{16,48},{32,64},{48,80},{64,96},{80,112},{96,128},{112,144}... | collective-permute-start | bytes 393224 | tf_op jit(solution)/shard_map/ppermute | solution.py:201
  38.3 6.4 %collective-permute-start.3 = (bf16[8,32,256]{2,1,0:T(8,128)(2,1)S(1)}, bf16[8,32,256]{2,1,0:T(8,128)(2,1)S(1)}, u32[]{:S(2)}, u32[]{:S(2)}) collective-permute-start(bf16[8,32,256]{2,1,0:T(8,128)(2,1)S(1)} %get-tuple-element.6), channel_id=1, source_target_pairs={{32,0},{48,16},{64,32},{80,48},{96,64},{112,80},{128,96},{144,112}... | collective-permute-start | bytes 393224 | tf_op jit(solution)/shard_map/ppermute | solution.py:202
  40.7 6.5 %collective-permute-start = (bf16[8,32,256]{2,1,0:T(8,128)(2,1)S(1)}, bf16[8,32,256]{2,1,0:T(8,128)(2,1)S(1)}, u32[]{:S(2)}, u32[]{:S(2)}) collective-permute-start(bf16[8,32,256]{2,1,0:T(8,128)(2,1)S(1)} %get-tuple-element.8), channel_id=1, source_target_pairs={{0,32},{16,48},{32,64},{48,80},{64,96},{80,112},{96,128},{112,144}... | collective-permute-start | bytes 393224 | tf_op jit(solution)/shard_map/ppermute | solution.py:201
  40.7 6.5 %collective-permute-start.1 = (bf16[8,32,256]{2,1,0:T(8,128)(2,1)S(1)}, bf16[8,32,256]{2,1,0:T(8,128)(2,1)S(1)}, u32[]{:S(2)}, u32[]{:S(2)}) collective-permute-start(bf16[8,32,256]{2,1,0:T(8,128)(2,1)S(1)} %get-tuple-element.5), channel_id=1, source_target_pairs={{32,0},{48,16},{64,32},{80,48},{96,64},{112,80},{128,96},{144,112}... | collective-permute-start | bytes 393224 | tf_op jit(solution)/shard_map/ppermute | solution.py:202

commit v4 on v3

v4 whole, which is shorter than its diff:
```python
import functools

import jax
import jax.numpy as jnp
from jax import lax
from jax.experimental import pallas as pl
from jax.experimental.pallas import tpu as pltpu
from jax.sharding import PartitionSpec as P

STEPS = 8
LANES = 128
THERE = (1, 4, 6, 12, 2, 8, 11, 14, 0, 10, 9, 13, 3, 7, 5, 15)
BACK = (1, 7, 6, 12, 2, 8, 11, 14, 0, 10, 9, 13, 3, 4, 5, 15)
SPLITS = 2


def place(piece, shard, pieces):
    return piece + (shard % 2) * (pieces - 1 - 2 * piece)


def loop_pairs(groups, shards, members):
    pieces = groups // members
    pairs = []
    for shard in range(shards):
        for piece in range(pieces):
            for member in range(members):
                carry, after = divmod(piece + 1, pieces)
                then = (shard + carry) % shards
                here = place(piece, shard, pieces) * members + member
                there = place(after, then, pieces) * members + member
                pairs.append((here * shards + shard, there * shards + then))
    return pairs


def slot(order, member, piece, members):
    return order.index(piece * members + member)


def owners(order, shard, pieces, members):
    return [place(cell // members, shard, pieces) * members + cell % members for cell in order]


def exchange(order, blocks, groups, shards, members):
    devices = [[lev * shards + shard for lev in owners(order, shard, groups // members, members)] for shard in range(shards)]
    return lax.all_to_all(blocks, ("lev", "lon"), 0, 0, tiled=True, axis_index_groups=devices)


def basis_by_owner(order, basis, groups, members):
    rows = basis.shape[0] // groups

    def ordered(shard):
        found = owners(order, shard, groups // members, members)
        return jnp.concatenate([basis[lev * rows : (lev + 1) * rows] for lev in found])

    return jnp.where(lax.axis_index("lon") % 2 == 0, ordered(0), ordered(1))


def pack_kernel(pieces, field_ref, out_ref):
    members, levels, lons, lats = field_ref.shape
    width = lons // pieces
    for level in range(levels):
        for member in range(members):
            for piece in range(pieces):
                out_ref[slot(THERE, member, piece, members), level * width : (level + 1) * width, :] = field_ref[
                    member, level, piece * width : (piece + 1) * width, :
                ]


def pack(field, pieces):
    members, levels, lons, lats = field.shape
    return pl.pallas_call(
        functools.partial(pack_kernel, pieces),
        out_shape=jax.ShapeDtypeStruct((pieces * members, levels * (lons // pieces), lats), field.dtype),
        in_specs=[pl.BlockSpec(memory_space=pltpu.VMEM)],
        out_specs=pl.BlockSpec(memory_space=pltpu.VMEM),
        compiler_params=pltpu.CompilerParams(vmem_limit_bytes=16 * 1024 * 1024),
        name="pack",
    )(field)


def unpack_kernel(pieces, blocks_ref, out_ref, held_ref, sems):
    members, levels, lons, lats = out_ref.shape
    width = lons // pieces
    copies = []
    for level in range(levels):
        for member in range(members):
            for piece in range(pieces):
                at = slot(BACK, member, piece, members)
                for half in range(lats // LANES):
                    row = (half * levels + level) * width
                    columns = slice(half * LANES, (half + 1) * LANES)
                    held_ref[member, level, piece * width : (piece + 1) * width, columns] = blocks_ref[at, row : row + width, :]
            copy = pltpu.make_async_copy(held_ref.at[member, level], out_ref.at[member, level], sems.at[member, level])
            copy.start()
            copies.append(copy)
    for copy in copies:
        copy.wait()


def unpack(blocks, shape, pieces):
    members, levels, lons, lats = shape
    return pl.pallas_call(
        functools.partial(unpack_kernel, pieces),
        out_shape=jax.ShapeDtypeStruct(shape, blocks.dtype),
        in_specs=[pl.BlockSpec(memory_space=pltpu.VMEM)],
        out_specs=pl.BlockSpec(memory_space=pl.ANY),
        scratch_shapes=[pltpu.VMEM(shape, blocks.dtype), pltpu.SemaphoreType.DMA((members, levels))],
        compiler_params=pltpu.CompilerParams(vmem_limit_bytes=16 * 1024 * 1024),
        name="unpack",
    )(blocks)


def paired(lats):
    row = lax.broadcasted_iota(jnp.int32, (lats, lats), 0)
    column = lax.broadcasted_iota(jnp.int32, (lats, lats), 1)
    half = lats // 2
    to = jnp.where(column < half, 2 * column, 2 * (column - half) + 1)
    back = jnp.where(row < half, 2 * row, 2 * (row - half) + 1)
    spread = jnp.where(row == to, 1.0, 0.0).astype(jnp.bfloat16)
    gather = jnp.where(column == back, 1.0, 0.0).astype(jnp.bfloat16)
    return spread, gather


def diffuse(modes_ref, left_ref, right_ref, kappa_ref, out_ref, u_ref, v_ref):
    width, count, lats = modes_ref.shape
    half = lats // 2
    total = width + 2 * STEPS
    spread, gather = paired(lats)

    def load(ref, at):
        cells = ref[...].reshape(ref.shape[0] * count, lats)
        cells = jnp.dot(cells, spread, preferred_element_type=jnp.float32)
        u_ref[at : at + ref.shape[0]] = cells.reshape(ref.shape[0], count, lats)

    load(left_ref, 0)
    load(modes_ref, STEPS)
    load(right_ref, STEPS + width)
    lane = lax.broadcasted_iota(jnp.int32, (count, half), 1)
    first, last = lane == 0, lane == half - 1
    kappa = kappa_ref[:, :half], kappa_ref[:, half:]
    keep = 1.0 - 4.0 * kappa[0], 1.0 - 4.0 * kappa[1]
    old, new = u_ref, v_ref
    for step in range(STEPS):
        before = old[step, :, :half], old[step, :, half:]
        here = old[step + 1, :, :half], old[step + 1, :, half:]
        for column in range(step + 1, total - step - 1):
            after = old[column + 1, :, :half], old[column + 1, :, half:]
            even, odd = here
            beside_even = odd + jnp.where(first, 0.0, pltpu.roll(odd, 1, 1))
            beside_odd = even + jnp.where(last, 0.0, pltpu.roll(even, half - 1, 1))
            new[column, :, :half] = keep[0] * even + kappa[0] * ((before[0] + after[0]) + beside_even)
            new[column, :, half:] = keep[1] * odd + kappa[1] * ((before[1] + after[1]) + beside_odd)
            before, here = here, after
        old, new = new, old
    cells = old[STEPS : STEPS + width].astype(jnp.bfloat16).reshape(width * count, lats)
    cells = jnp.dot(cells, gather, preferred_element_type=jnp.float32)
    out_ref[...] = cells.astype(out_ref.dtype).reshape(width, count, lats)


def diffused(modes, left, right, kappa):
    width, count, lats = modes.shape
    cells = pltpu.VMEM((width + 2 * STEPS, count, lats), jnp.float32)
    return pl.pallas_call(
        diffuse,
        out_shape=jax.ShapeDtypeStruct(modes.shape, jnp.bfloat16),
        in_specs=[pl.BlockSpec(memory_space=pltpu.VMEM)] * 4,
        out_specs=pl.BlockSpec(memory_space=pltpu.VMEM),
        scratch_shapes=[cells, cells],
        compiler_params=pltpu.CompilerParams(vmem_limit_bytes=16 * 1024 * 1024),
        cost_estimate=pl.CostEstimate(flops=60 * count * lats * (width + STEPS), bytes_accessed=6 * count * lats * width, transcendentals=0),
        name="diffuse",
    )(modes, left, right, kappa)


def on_device(field, eof_basis, band_of_mode, coef_table):
    groups, shards = lax.axis_size("lev"), lax.axis_size("lon")
    members, levels, lons, lats = field.shape
    pieces = groups // members
    width = lons // pieces
    count = eof_basis.shape[1]
    basis = basis_by_owner(THERE, eof_basis, groups, members)
    basis_back = basis_by_owner(BACK, eof_basis, groups, members)
    cut = pack(field, pieces)
    whole = exchange(THERE, cut, groups, shards, members).reshape(groups * levels, width, lats)
    modes = jnp.einsum("lk,lxy->xky", basis, whole, preferred_element_type=jnp.float32).astype(jnp.bfloat16)
    onward = loop_pairs(groups, shards, members)
    back = [(b, a) for a, b in onward]
    onehot = (band_of_mode[:, None] == jnp.arange(coef_table.shape[0])[None, :]).astype(jnp.float32)
    pairs = coef_table.reshape(-1, lats // 2, 2).transpose(0, 2, 1).reshape(coef_table.shape)
    kappa = jnp.dot(onehot, pairs, precision=lax.Precision.HIGHEST)
    share = count // SPLITS
    parts = []
    for split in range(SPLITS):
        some = modes[:, split * share : (split + 1) * share]
        left = lax.ppermute(some[width - STEPS :], ("lev", "lon"), onward)
        right = lax.ppermute(some[:STEPS], ("lev", "lon"), back)
        parts.append(diffused(some, left, right, kappa[split * share : (split + 1) * share]))
    final = jnp.concatenate(parts, axis=1) if SPLITS > 1 else parts[0]
    total = jnp.einsum("lk,xky->lxy", basis_back, final, preferred_element_type=jnp.float32).astype(jnp.bfloat16)
    total = total.reshape(groups, levels * width, lats // LANES, LANES).transpose(0, 2, 1, 3).reshape(groups, -1, LANES)
    total = exchange(BACK, total, groups, shards, members)
    return unpack(total, field.shape, pieces)


def solution(mesh):
    return jax.shard_map(
        on_device,
        mesh=mesh,
        in_specs=(P(None, "lev", "lon", None), P(), P(), P()),
        out_specs=P(None, "lev", "lon", None),
        check_vma=False,
    )
```

time: 82.4 us -> 80.7 us (0.979); the launches traced: 82.1 us -> 79.5 us
  waiting for transfers between devices: 24.3 us -> 22.8 us
  Pallas kernels: 7.09 us -> 5.67 us
  blocking collectives: 30.3 us -> 29 us
  local copies, waits for them, and re-layouts: 2.47 us -> 3.66 us
    ppermute x2, starting transfers between devices: 5.07 us -> 1.22 us  [on_device(): right = lax.ppermute(some[:STEPS], ('lev', 'lon'), back)]
    ppermute x2, starting transfers between devices: 0.31 us -> 4.16 us  [on_device(): left = lax.ppermute(some[width - STEPS:], ('lev', 'lon'), onward)]
    all_to_all x1, waiting for transfers between devices: 23 us -> 20.6 us  [exchange(): lax.all_to_all(blocks, ('lev', 'lon'), 0, 0, tiled=True, axis_index_group...]
    pallas_call x2, Pallas kernels: 5.01 us -> 3.59 us  [diffused(): pl.pallas_call(diffuse, out_shape=jax.ShapeDtypeStruct(modes.shape, jnp.b...]
    all_to_all x1, blocking collectives: 30.3 us -> 29 us  [exchange(): lax.all_to_all(blocks, ('lev', 'lon'), 0, 0, tiled=True, axis_index_group...]
  transfers between devices with their start and end apart: 5 -> 5, of which waited for: 3 -> 4; matrix products, arithmetic and copies ran while one was open for 1% -> 2% of each run, Pallas kernels for 3% -> 2%
where the time goes in v4:
time: 80.7 us; the launch traced here: 79.5 us
  blocking collectives  29 us (36%)
  waiting for transfers between devices  22.8 us (28%)
  starting transfers between devices  17.2 us (21%)
  Pallas kernels  5.67 us (7%)
  local copies, waits for them, and re-layouts  3.66 us (5%)
  matrix products  1.05 us (1%)
    all_to_all x1, blocking collectives, exchange(): lax.all_to_all(blocks, ('lev', 'lon'), 0, 0, tiled=True, axis_index_group...  29 us
    all_to_all x1, waiting for transfers between devices, exchange(): lax.all_to_all(blocks, ('lev', 'lon'), 0, 0, tiled=True, axis_index_group...  20.6 us
    all_to_all x1, starting transfers between devices, exchange(): lax.all_to_all(blocks, ('lev', 'lon'), 0, 0, tiled=True, axis_index_group...  11.8 us
    ppermute x2, starting transfers between devices, on_device(): left = lax.ppermute(some[width - STEPS:], ('lev', 'lon'), onward)  4.16 us
    pallas_call x2, Pallas kernels, diffused(): pl.pallas_call(diffuse, out_shape=jax.ShapeDtypeStruct(modes.shape, jnp.b...  3.59 us
  transfers between devices with their start and end apart: 5, of which 4 were waited for; matrix products, arithmetic and copies ran while one was open for 2% of the time, Pallas kernels for 2%

profile of v4, /device:TPU:2, one launch (start us, length us, event | category | flops | bytes accessed | tf_op | source)
XLA Modules:
  0.0 79.5 jit_solution(14827326380442866651)
XLA Ops:
  0.0 1.2 %copy-done = bf16[2,9,96,256]{3,2,1,0:T(8,128)(2,1)S(1)} copy-done((bf16[2,9,96,256]{3,2,1,0:T(8,128)(2,1)S(1)}, bf16[2,9,96,256]{3,2,1,0:T(8,128)(2,1)}, u32[]{:S(2)}) %copy-start) | copy-done | bytes 884760
  1.2 1.0 %pack.1 = bf16[16,108,256]{2,1,0:T(8,128)(2,1)} custom-call(bf16[2,9,96,256]{3,2,1,0:T(8,128)(2,1)S(1)} %copy-done), custom_call_target="tpu_custom_call" | custom-call | tf_op jit(solution)/shard_map/pack/pallas_call | solution.py:71
  2.2 11.8 %all-to-all-start = ((bf16[16,108,256]{2,1,0:T(8,128)(2,1)}), bf16[16,108,256]{2,1,0:T(8,128)(2,1)S(1)}, u32[]{:S(2)}, u32[]{:S(2)}) async-start(bf16[16,108,256]{2,1,0:T(8,128)(2,1)} %pack.1), calls=%async_computation | async-start | bytes 1835008 | tf_op jit(solution)/shard_map/all_to_all | solution.py:45
  14.0 0.1 fusion.18
  14.2 0.2 concatenate.19
  14.3 0.2 concatenate.20
  14.5 0.1 slice.70
  14.6 0.1 slice.147
  14.6 0.1 copy.7
  14.8 0.1 copy.8
  14.8 0.2 concatenate.17
  15.0 0.1 concatenate.18
  15.2 0.2 fusion.9
  15.4 20.6 %all-to-all-done = bf16[16,108,256]{2,1,0:T(8,128)(2,1)S(1)} async-done(((bf16[16,108,256]{2,1,0:T(8,128)(2,1)}), bf16[16,108,256]{2,1,0:T(8,128)(2,1)S(1)}, u32[]{:S(2)}, u32[]{:S(2)}) %all-to-all-start) | async-done | bytes 884768 | tf_op jit(solution)/shard_map/all_to_all | solution.py:45
  36.0 0.2 reshape.16
  36.3 0.4 fusion
  36.7 2.4 %collective-permute-start.2 = (bf16[8,32,256]{2,1,0:T(8,128)(2,1)S(1)}, bf16[8,32,256]{2,1,0:T(8,128)(2,1)S(1)}, u32[]{:S(2)}, u32[]{:S(2)}) collective-permute-start(bf16[8,32,256]{2,1,0:T(8,128)(2,1)S(1)} %get-tuple-element.7), channel_id=1, source_target_pairs={{0,32},{16,48},{32,64},{48,80},{64,96},{80,112},{96,128},{112,144}... | collective-permute-start | bytes 393224 | tf_op jit(solution)/shard_map/ppermute | solution.py:195
  39.2 0.3 collective-permute-start.3
  39.5 1.7 %collective-permute-start = (bf16[8,32,256]{2,1,0:T(8,128)(2,1)S(1)}, bf16[8,32,256]{2,1,0:T(8,128)(2,1)S(1)}, u32[]{:S(2)}, u32[]{:S(2)}) collective-permute-start(bf16[8,32,256]{2,1,0:T(8,128)(2,1)S(1)} %get-tuple-element.8), channel_id=1, source_target_pairs={{0,32},{16,48},{32,64},{48,80},{64,96},{80,112},{96,128},{112,144}... | collective-permute-start | bytes 393224 | tf_op jit(solution)/shard_map/ppermute | solution.py:195
  41.2 0.9 %collective-permute-start.1 = (bf16[8,32,256]{2,1,0:T(8,128)(2,1)S(1)}, bf16[8,32,256]{2,1,0:T(8,128)(2,1)S(1)}, u32[]{:S(2)}, u32[]{:S(2)}) collective-permute-start(bf16[8,32,256]{2,1,0:T(8,128)(2,1)S(1)} %get-tuple-element.5), channel_id=1, source_target_pairs={{32,0},{48,16},{64,32},{80,48},{96,64},{112,80},{128,96},{144,112}... | collective-permute-start | bytes 393224 | tf_op jit(solution)/shard_map/ppermute | solution.py:196
  42.1 0.7 collective-permute-done.2.left_ref
  42.8 1.3 %collective-permute-done.3.right_ref = bf16[8,32,256]{2,1,0:T(8,128)(2,1)S(1)} collective-permute-done((bf16[8,32,256]{2,1,0:T(8,128)(2,1)S(1)}, bf16[8,32,256]{2,1,0:T(8,128)(2,1)S(1)}, u32[]{:S(2)}, u32[]{:S(2)}) %collective-permute-start.3) | collective-permute-done | bytes 131104 | tf_op jit(solution)/shard_map/ppermute | solution.py:196
  44.1 1.8 %diffuse.3 = bf16[12,32,256]{2,1,0:T(8,128)(2,1)S(1)} custom-call(bf16[12,32,256]{2,1,0:T(8,128)(2,1)S(1)} %get-tuple-element.10.modes_ref, bf16[8,32,256]{2,1,0:T(8,128)(2,1)S(1)} %collective-permute-done.2.left_ref, bf16[8,32,256]{2,1,0:T(8,128)(2,1)S(1)} %collective-permute-done.3.right_ref, f32[32,256]{1,0:T(8,128)S(1)} %get-tuple-element.12.kappa_ref), custom_call_target="tpu_custom_call" | custom-call | flops 9830400 | bytes 589824 | tf_op jit(solution)/shard_map/diffuse/pallas_call | solution.py:163
  45.9 0.2 collective-permute-done.1.right_ref
  46.2 1.8 %diffuse.2 = bf16[12,32,256]{2,1,0:T(8,128)(2,1)S(1)} custom-call(bf16[12,32,256]{2,1,0:T(8,128)(2,1)S(1)} %get-tuple-element.9.modes_ref, bf16[8,32,256]{2,1,0:T(8,128)(2,1)S(1)} %collective-permute-done.left_ref, bf16[8,32,256]{2,1,0:T(8,128)(2,1)S(1)} %collective-permute-done.1.right_ref, f32[32,256]{1,0:T(8,128)S(1)} %get-tuple-element.11.kappa_ref), custom_call_target="tpu_custom_call" | custom-call | flops 9830400 | bytes 589824 | tf_op jit(solution)/shard_map/diffuse/pallas_call | solution.py:163
  48.0 0.4 convolution_convert_fusion
  48.4 0.3 copy.9
  48.7 0.4 reshape.19
  49.1 0.1 copy.10
  49.3 0.2 copy.11
  49.5 29.0 %all_to_all.10.blocks_ref = bf16[16,216,128]{2,1,0:T(8,128)(2,1)S(1)} all-to-all(bf16[16,216,128]{2,1,0:T(8,128)(2,1)S(1)} %copy.11), channel_id=1, replica_groups={{16,112,96,192,32,128,176,224,0,160,144,208,48,64,80,240},{241,145,129,..., dimensions={0} | all-to-all | bytes 1769472 | tf_op jit(solution)/shard_map/all_to_all | solution.py:45
  78.5 1.1 %unpack.1 = bf16[2,9,96,256]{3,2,1,0:T(8,128)(2,1)} custom-call(bf16[16,216,128]{2,1,0:T(8,128)(2,1)S(1)} %all_to_all.10.blocks_ref), custom_call_target="tpu_custom_call" | custom-call | tf_op jit(solution)/shard_map/unpack/pallas_call | solution.py:102
  (11 shorter events, 0.1 us)
Async XLA Ops:
  0.0 1.2 %copy-start = (bf16[2,9,96,256]{3,2,1,0:T(8,128)(2,1)S(1)}, bf16[2,9,96,256]{3,2,1,0:T(8,128)(2,1)}, u32[]{:S(2)}) copy-start(bf16[2,9,96,256]{3,2,1,0:T(8,128)(2,1)} %field_ref.1) | copy-start | bytes 2654212
  2.2 11.8 %copy-start.1 = (bf16[144,64]{0,1:T(8,128)(2,1)S(1)}, bf16[144,64]{0,1:T(8,128)(2,1)}, u32[]{:S(2)}) copy-start(bf16[144,64]{0,1:T(8,128)(2,1)} %param.5) | copy-start | bytes 55300
  2.2 12.5 %copy-start.2 = (f32[8,256]{1,0:T(8,128)S(1)}, f32[8,256]{1,0:T(8,128)}, u32[]{:S(2)}) copy-start(f32[8,256]{1,0:T(8,128)} %param.7) | copy-start | bytes 24580
  2.2 33.8 %all-to-all-start = ((bf16[16,108,256]{2,1,0:T(8,128)(2,1)}), bf16[16,108,256]{2,1,0:T(8,128)(2,1)S(1)}, u32[]{:S(2)}, u32[]{:S(2)}) async-start(bf16[16,108,256]{2,1,0:T(8,128)(2,1)} %pack.1), calls=%async_computation | async-start | bytes 1835008 | tf_op jit(solution)/shard_map/all_to_all | solution.py:45
  14.0 1.2 %copy-start.3 = (s32[64]{0:T(128)S(1)}, s32[64]{0:T(128)}, u32[]{:S(2)}) copy-start(s32[64]{0:T(128)} %param.6) | copy-start | bytes 772
  36.7 6.1 %collective-permute-start.2 = (bf16[8,32,256]{2,1,0:T(8,128)(2,1)S(1)}, bf16[8,32,256]{2,1,0:T(8,128)(2,1)S(1)}, u32[]{:S(2)}, u32[]{:S(2)}) collective-permute-start(bf16[8,32,256]{2,1,0:T(8,128)(2,1)S(1)} %get-tuple-element.7), channel_id=1, source_target_pairs={{0,32},{16,48},{32,64},{48,80},{64,96},{80,112},{96,128},{112,144}... | collective-permute-start | bytes 393224 | tf_op jit(solution)/shard_map/ppermute | solution.py:195
  39.2 5.0 %collective-permute-start.3 = (bf16[8,32,256]{2,1,0:T(8,128)(2,1)S(1)}, bf16[8,32,256]{2,1,0:T(8,128)(2,1)S(1)}, u32[]{:S(2)}, u32[]{:S(2)}) collective-permute-start(bf16[8,32,256]{2,1,0:T(8,128)(2,1)S(1)} %get-tuple-element.6), channel_id=1, source_target_pairs={{32,0},{48,16},{64,32},{80,48},{96,64},{112,80},{128,96},{144,112}... | collective-permute-start | bytes 393224 | tf_op jit(solution)/shard_map/ppermute | solution.py:196
  39.5 6.5 %collective-permute-start = (bf16[8,32,256]{2,1,0:T(8,128)(2,1)S(1)}, bf16[8,32,256]{2,1,0:T(8,128)(2,1)S(1)}, u32[]{:S(2)}, u32[]{:S(2)}) collective-permute-start(bf16[8,32,256]{2,1,0:T(8,128)(2,1)S(1)} %get-tuple-element.8), channel_id=1, source_target_pairs={{0,32},{16,48},{32,64},{48,80},{64,96},{80,112},{96,128},{112,144}... | collective-permute-start | bytes 393224 | tf_op jit(solution)/shard_map/ppermute | solution.py:195
  41.2 5.0 %collective-permute-start.1 = (bf16[8,32,256]{2,1,0:T(8,128)(2,1)S(1)}, bf16[8,32,256]{2,1,0:T(8,128)(2,1)S(1)}, u32[]{:S(2)}, u32[]{:S(2)}) collective-permute-start(bf16[8,32,256]{2,1,0:T(8,128)(2,1)S(1)} %get-tuple-element.5), channel_id=1, source_target_pairs={{32,0},{48,16},{64,32},{80,48},{96,64},{112,80},{128,96},{144,112}... | collective-permute-start | bytes 393224 | tf_op jit(solution)/shard_map/ppermute | solution.py:196

commit v5 on v4

--- a/solution.py
+++ b/solution.py
@@ -61,16 +61,18 @@
     for level in range(levels):
         for member in range(members):
             for piece in range(pieces):
-                out_ref[slot(THERE, member, piece, members), level * width : (level + 1) * width, :] = field_ref[
-                    member, level, piece * width : (piece + 1) * width, :
-                ]
+                to = slot(THERE, member, piece, members)
+                for half in range(lats // LANES):
+                    row = (half * levels + level) * width
+                    columns = slice(half * LANES, (half + 1) * LANES)
+                    out_ref[to, row : row + width, :] = field_ref[member, level, piece * width : (piece + 1) * width, columns]
 
 
 def pack(field, pieces):
     members, levels, lons, lats = field.shape
     return pl.pallas_call(
         functools.partial(pack_kernel, pieces),
-        out_shape=jax.ShapeDtypeStruct((pieces * members, levels * (lons // pieces), lats), field.dtype),
+        out_shape=jax.ShapeDtypeStruct((pieces * members, levels * (lons // pieces) * lats // LANES, LANES), field.dtype),
         in_specs=[pl.BlockSpec(memory_space=pltpu.VMEM)],
         out_specs=pl.BlockSpec(memory_space=pltpu.VMEM),
         compiler_params=pltpu.CompilerParams(vmem_limit_bytes=16 * 1024 * 1024),
@@ -108,6 +110,75 @@
         compiler_params=pltpu.CompilerParams(vmem_limit_bytes=16 * 1024 * 1024),
         name="unpack",
     )(blocks)
+
+
+def doubled(basis, groups):
+    rows = basis.reshape(groups, 1, -1, 1, basis.shape[1])
+    same = jnp.eye(2, dtype=basis.dtype).reshape(1, 2, 1, 2, 1)
+    return (rows * same).reshape(2 * basis.shape[0], 2 * basis.shape[1])
+
+
+def project_kernel(width, blocks_ref, basis_ref, *refs):
+    outs, held_ref = refs[:-1], refs[-1]
+    groups, rows, lanes = blocks_ref.shape
+    modes = basis_ref.shape[0] // 2
+    share = modes // SPLITS
+    for block in range(groups):
+        held_ref[block * rows : (block + 1) * rows, :] = blocks_ref[block].astype(jnp.float32)
+    for column in range(width):
+        levels = held_ref[pl.ds(column, groups * rows // width, stride=width), :].astype(jnp.bfloat16)
+        cells = jnp.dot(basis_ref[...], levels, preferred_element_type=jnp.float32).astype(jnp.bfloat16)
+        cells = jnp.concatenate([cells[:modes], cells[modes:]], axis=1)
+        for split in range(SPLITS):
+            part = cells[split * share : (split + 1) * share]
+            whole_ref, tail_ref, head_ref = outs[3 * split : 3 * split + 3]
+            whole_ref[column] = part
+            if column >= width - STEPS:
+                tail_ref[column - width + STEPS] = part
+            if column < STEPS:
+                head_ref[column] = part
+
+
+def project(blocks, basis, width):
+    groups, rows, lanes = blocks.shape
+    share = basis.shape[0] // 2 // SPLITS
+    shapes = [jax.ShapeDtypeStruct((columns, share, 2 * lanes), jnp.bfloat16) for columns in (width, STEPS, STEPS)]
+    return pl.pallas_call(
+        functools.partial(project_kernel, width),
+        out_shape=shapes * SPLITS,
+        in_specs=[pl.BlockSpec(memory_space=pltpu.VMEM)] * 2,
+        out_specs=[pl.BlockSpec(memory_space=pltpu.VMEM)] * (3 * SPLITS),
+        scratch_shapes=[pltpu.VMEM((groups * rows, lanes), jnp.float32)],
+        compiler_params=pltpu.CompilerParams(vmem_limit_bytes=16 * 1024 * 1024),
+        name="project",
+    )(blocks, basis)
+
+
+def expand_kernel(groups, basis_ref, *refs):
+    parts, out_ref, held_ref = refs[:SPLITS], refs[SPLITS], refs[SPLITS + 1]
+    width = parts[0].shape[0]
+    rows, lanes = out_ref.shape[1:]
+    for column in range(width):
+        cells = [part[column, :, half * lanes : (half + 1) * lanes] for half in range(2) for part in parts]
+        cells = jnp.concatenate(cells, axis=0)
+        levels = jnp.dot(basis_ref[...], cells, preferred_element_type=jnp.float32)
+        held_ref[pl.ds(column, groups * rows // width, stride=width), :] = levels
+    for block in range(groups):
+        out_ref[block] = held_ref[block * rows : (block + 1) * rows, :].astype(out_ref.dtype)
+
+
+def expand(parts, basis, groups):
+    width, share, lats = parts[0].shape
+    rows = basis.shape[0] * width // groups
+    return pl.pallas_call(
+        functools.partial(expand_kernel, groups),
+        out_shape=jax.ShapeDtypeStruct((groups, rows, lats // 2), jnp.bfloat16),
+        in_specs=[pl.BlockSpec(memory_space=pltpu.VMEM)] * (SPLITS + 1),
+        out_specs=pl.BlockSpec(memory_space=pltpu.VMEM),
+        scratch_shapes=[pltpu.VMEM((groups * rows, lats // 2), jnp.float32)],
+        compiler_params=pltpu.CompilerParams(vmem_limit_bytes=16 * 1024 * 1024),
+        name="expand",
+    )(basis, *parts)
 
 
 def paired(lats):
@@ -181,8 +252,8 @@
     basis = basis_by_owner(THERE, eof_basis, groups, members)
     basis_back = basis_by_owner(BACK, eof_basis, groups, members)
     cut = pack(field, pieces)
-    whole = exchange(THERE, cut, groups, shards, members).reshape(groups * levels, width, lats)
-    modes = jnp.einsum("lk,lxy->xky", basis, whole, preferred_element_type=jnp.float32).astype(jnp.bfloat16)
+    whole = exchange(THERE, cut, groups, shards, members)
+    modes = project(whole, doubled(basis, groups).T, width)
     onward = loop_pairs(groups, shards, members)
     back = [(b, a) for a, b in onward]
     onehot = (band_of_mode[:, None] == jnp.arange(coef_table.shape[0])[None, :]).astype(jnp.float32)
@@ -191,13 +262,11 @@
     share = count // SPLITS
     parts = []
     for split in range(SPLITS):
-        some = modes[:, split * share : (split + 1) * share]
-        left = lax.ppermute(some[width - STEPS :], ("lev", "lon"), onward)
-        right = lax.ppermute(some[:STEPS], ("lev", "lon"), back)
+        some, tail, head = modes[3 * split : 3 * split + 3]
+        left = lax.ppermute(tail, ("lev", "lon"), onward)
+        right = lax.ppermute(head, ("lev", "lon"), back)
         parts.append(diffused(some, left, right, kappa[split * share : (split + 1) * share]))
-    final = jnp.concatenate(parts, axis=1) if SPLITS > 1 else parts[0]
-    total = jnp.einsum("lk,xky->lxy", basis_back, final, preferred_element_type=jnp.float32).astype(jnp.bfloat16)
-    total = total.reshape(groups, levels * width, lats // LANES, LANES).transpose(0, 2, 1, 3).reshape(groups, -1, LANES)
+    total = expand(parts, doubled(basis_back, groups), groups)
     total = exchange(BACK, total, groups, shards, members)
     return unpack(total, field.shape, pieces)
 

time: 80.7 us -> 79 us (0.979)
  waiting for transfers between devices: 22.8 us -> 20 us
  Pallas kernels: 5.67 us -> 6.86 us
  matrix products: 1.05 us -> 0.22 us
    all_to_all x1, waiting for transfers between devices: 20.6 us -> 17.8 us  [exchange(): lax.all_to_all(blocks, ('lev', 'lon'), 0, 0, tiled=True, axis_index_group...]
    unnamed x9, local copies, waits for them, and re-layouts: 1.3 us -> 2.45 us
    pallas_call x0 -> x2, Pallas kernels: none -> 1.03 us  [the longest x1 0.58 us: project(): pl.pallas_call(functools.partial(project_kernel, width), out_shape=shapes...]
    reshape x3 -> x0, local copies, waits for them, and re-layouts: 0.87 us -> none  [the longest x2 0.66 us: on_device(): total.reshape(groups, levels * width, lats // LANES, LANES)]
    dot_general x2 -> x0, matrix products: 0.83 us -> none  [the longest x1 0.42 us: on_device(): jnp.einsum('lk,xky->lxy', basis_back, final, preferred_element_type=jnp.f...]
  transfers between devices with their start and end apart: 5 -> 5, of which waited for: 4 -> 4; matrix products, arithmetic and copies ran while one was open for 2% -> 3% of each run, Pallas kernels for 2% -> 2%
where the time goes in v5:
time: 79 us; the launch traced here: 78 us
  blocking collectives  29.2 us (37%)
  waiting for transfers between devices  20 us (25%)
  starting transfers between devices  17.2 us (22%)
  Pallas kernels  6.86 us (9%)
  local copies, waits for them, and re-layouts  4.02 us (5%)
    all_to_all x1, blocking collectives, exchange(): lax.all_to_all(blocks, ('lev', 'lon'), 0, 0, tiled=True, axis_index_group...  29.2 us
    all_to_all x1, waiting for transfers between devices, exchange(): lax.all_to_all(blocks, ('lev', 'lon'), 0, 0, tiled=True, axis_index_group...  17.8 us
    all_to_all x1, starting transfers between devices, exchange(): lax.all_to_all(blocks, ('lev', 'lon'), 0, 0, tiled=True, axis_index_group...  11.8 us
    ppermute x2, starting transfers between devices, on_device(): left = lax.ppermute(tail, ('lev', 'lon'), onward)  4.16 us
    pallas_call x2, Pallas kernels, diffused(): pl.pallas_call(diffuse, out_shape=jax.ShapeDtypeStruct(modes.shape, jnp.b...  3.59 us
    unnamed x9, local copies, waits for them, and re-layouts  2.45 us
  transfers between devices with their start and end apart: 5, of which 4 were waited for; matrix products, arithmetic and copies ran while one was open for 3% of the time, Pallas kernels for 2%

profile of v5, /device:TPU:2, one launch (start us, length us, event | category | flops | bytes accessed | tf_op | source)
XLA Modules:
  0.0 78.0 jit_solution(2959010565017511204)
XLA Ops:
  0.0 1.2 %copy-done = bf16[2,9,96,256]{3,2,1,0:T(8,128)(2,1)S(1)} copy-done((bf16[2,9,96,256]{3,2,1,0:T(8,128)(2,1)S(1)}, bf16[2,9,96,256]{3,2,1,0:T(8,128)(2,1)}, u32[]{:S(2)}) %copy-start) | copy-done | bytes 884760
  1.2 1.2 %pack.1 = bf16[16,216,128]{2,1,0:T(8,128)(2,1)} custom-call(bf16[2,9,96,256]{3,2,1,0:T(8,128)(2,1)S(1)} %copy-done), custom_call_target="tpu_custom_call" | custom-call | tf_op jit(solution)/shard_map/pack/pallas_call | solution.py:73
  2.3 11.8 %all-to-all-start = ((bf16[16,216,128]{2,1,0:T(8,128)(2,1)}), bf16[16,216,128]{2,1,0:T(8,128)(2,1)S(1)}, u32[]{:S(2)}, u32[]{:S(2)}) async-start(bf16[16,216,128]{2,1,0:T(8,128)(2,1)} %pack.1), calls=%async_computation | async-start | bytes 1769472 | tf_op jit(solution)/shard_map/all_to_all | solution.py:45
  14.2 0.1 fusion.4
  14.3 0.2 concatenate.16
  14.5 0.2 concatenate.17
  14.8 0.1 concatenate.14
  14.9 0.1 concatenate.15
  15.1 0.1 copy.9
  15.3 0.1 copy.8
  15.4 0.3 broadcast_multiply_fusion
  15.7 0.1 mul.37.basis_ref
  15.9 0.1 mul.40
  16.0 0.1 copy.10
  16.1 0.6 copy-done.2
  16.7 0.1 copy.11
  16.9 0.6 copy-done.3
  17.5 0.2 fusion
  17.7 17.8 %all-to-all-done.blocks_ref = bf16[16,216,128]{2,1,0:T(8,128)(2,1)S(1)} async-done(((bf16[16,216,128]{2,1,0:T(8,128)(2,1)}), bf16[16,216,128]{2,1,0:T(8,128)(2,1)S(1)}, u32[]{:S(2)}, u32[]{:S(2)}) %all-to-all-start) | async-done | bytes 884768 | tf_op jit(solution)/shard_map/all_to_all | solution.py:45
  35.5 0.6 project.1
  36.1 2.4 %collective-permute-start = (bf16[8,32,256]{2,1,0:T(8,128)(2,1)S(1)}, bf16[8,32,256]{2,1,0:T(8,128)(2,1)S(1)}, u32[]{:S(2)}, u32[]{:S(2)}) collective-permute-start(bf16[8,32,256]{2,1,0:T(8,128)(2,1)S(1)} %get-tuple-element.12), channel_id=1, source_target_pairs={{0,32},{16,48},{32,64},{48,80},{64,96},{80,112},{96,128},{112,144}... | collective-permute-start | bytes 393224 | tf_op jit(solution)/shard_map/ppermute | solution.py:266
  38.5 0.3 collective-permute-start.1
  38.8 1.7 %collective-permute-start.2 = (bf16[8,32,256]{2,1,0:T(8,128)(2,1)S(1)}, bf16[8,32,256]{2,1,0:T(8,128)(2,1)S(1)}, u32[]{:S(2)}, u32[]{:S(2)}) collective-permute-start(bf16[8,32,256]{2,1,0:T(8,128)(2,1)S(1)} %get-tuple-element.15), channel_id=1, source_target_pairs={{0,32},{16,48},{32,64},{48,80},{64,96},{80,112},{96,128},{112,144}... | collective-permute-start | bytes 393224 | tf_op jit(solution)/shard_map/ppermute | solution.py:266
  40.5 0.9 %collective-permute-start.3 = (bf16[8,32,256]{2,1,0:T(8,128)(2,1)S(1)}, bf16[8,32,256]{2,1,0:T(8,128)(2,1)S(1)}, u32[]{:S(2)}, u32[]{:S(2)}) collective-permute-start(bf16[8,32,256]{2,1,0:T(8,128)(2,1)S(1)} %get-tuple-element.16), channel_id=1, source_target_pairs={{32,0},{48,16},{64,32},{80,48},{96,64},{112,80},{128,96},{144,112}... | collective-permute-start | bytes 393224 | tf_op jit(solution)/shard_map/ppermute | solution.py:267
  41.5 0.7 collective-permute-done.left_ref
  42.1 1.3 %collective-permute-done.1.right_ref = bf16[8,32,256]{2,1,0:T(8,128)(2,1)S(1)} collective-permute-done((bf16[8,32,256]{2,1,0:T(8,128)(2,1)S(1)}, bf16[8,32,256]{2,1,0:T(8,128)(2,1)S(1)}, u32[]{:S(2)}, u32[]{:S(2)}) %collective-permute-start.1) | collective-permute-done | bytes 131104 | tf_op jit(solution)/shard_map/ppermute | solution.py:267
  43.5 1.8 %diffuse.2.refs_0_ = bf16[12,32,256]{2,1,0:T(8,128)(2,1)S(1)} custom-call(bf16[12,32,256]{2,1,0:T(8,128)(2,1)S(1)} %get-tuple-element.11.modes_ref, bf16[8,32,256]{2,1,0:T(8,128)(2,1)S(1)} %collective-permute-done.left_ref, bf16[8,32,256]{2,1,0:T(8,128)(2,1)S(1)} %collective-permute-done.1.right_ref, f32[32,256]{1,0:T(8,128)S(1)} %get-tuple-element.18.kappa_ref), custom_call_target="tpu_custom_call" | custom-call | flops 9830400 | bytes 589824 | tf_op jit(solution)/shard_map/diffuse/pallas_call | solution.py:234
  45.3 0.2 collective-permute-done.3.right_ref
  45.5 1.8 %diffuse.3.refs_1_ = bf16[12,32,256]{2,1,0:T(8,128)(2,1)S(1)} custom-call(bf16[12,32,256]{2,1,0:T(8,128)(2,1)S(1)} %get-tuple-element.14.modes_ref, bf16[8,32,256]{2,1,0:T(8,128)(2,1)S(1)} %collective-permute-done.2.left_ref, bf16[8,32,256]{2,1,0:T(8,128)(2,1)S(1)} %collective-permute-done.3.right_ref, f32[32,256]{1,0:T(8,128)S(1)} %get-tuple-element.17.kappa_ref), custom_call_target="tpu_custom_call" | custom-call | flops 9830400 | bytes 589824 | tf_op jit(solution)/shard_map/diffuse/pallas_call | solution.py:234
  47.3 0.5 expand.1
  47.8 29.2 %all_to_all.10.blocks_ref = bf16[16,216,128]{2,1,0:T(8,128)(2,1)S(1)} all-to-all(bf16[16,216,128]{2,1,0:T(8,128)(2,1)S(1)} %expand.1), channel_id=1, replica_groups={{16,112,96,192,32,128,176,224,0,160,144,208,48,64,80,240},{241,145,129,..., dimensions={0} | all-to-all | bytes 1769472 | tf_op jit(solution)/shard_map/all_to_all | solution.py:45
  76.9 1.1 %unpack.1 = bf16[2,9,96,256]{3,2,1,0:T(8,128)(2,1)} custom-call(bf16[16,216,128]{2,1,0:T(8,128)(2,1)S(1)} %all_to_all.10.blocks_ref), custom_call_target="tpu_custom_call" | custom-call | tf_op jit(solution)/shard_map/unpack/pallas_call | solution.py:104
  (14 shorter events, 0.3 us)
Async XLA Ops:
  0.0 1.2 %copy-start = (bf16[2,9,96,256]{3,2,1,0:T(8,128)(2,1)S(1)}, bf16[2,9,96,256]{3,2,1,0:T(8,128)(2,1)}, u32[]{:S(2)}) copy-start(bf16[2,9,96,256]{3,2,1,0:T(8,128)(2,1)} %field_ref.1) | copy-start | bytes 2654212
  2.3 11.8 %copy-start.1 = (bf16[144,64]{0,1:T(8,128)(2,1)S(1)}, bf16[144,64]{0,1:T(8,128)(2,1)}, u32[]{:S(2)}) copy-start(bf16[144,64]{0,1:T(8,128)(2,1)} %param.5) | copy-start | bytes 55300
  2.3 33.1 %all-to-all-start = ((bf16[16,216,128]{2,1,0:T(8,128)(2,1)}), bf16[16,216,128]{2,1,0:T(8,128)(2,1)S(1)}, u32[]{:S(2)}, u32[]{:S(2)}) async-start(bf16[16,216,128]{2,1,0:T(8,128)(2,1)} %pack.1), calls=%async_computation | async-start | bytes 1769472 | tf_op jit(solution)/shard_map/all_to_all | solution.py:45
  16.0 0.7 copy-start.2
  16.8 0.7 copy-start.3
  36.1 6.1 %collective-permute-start = (bf16[8,32,256]{2,1,0:T(8,128)(2,1)S(1)}, bf16[8,32,256]{2,1,0:T(8,128)(2,1)S(1)}, u32[]{:S(2)}, u32[]{:S(2)}) collective-permute-start(bf16[8,32,256]{2,1,0:T(8,128)(2,1)S(1)} %get-tuple-element.12), channel_id=1, source_target_pairs={{0,32},{16,48},{32,64},{48,80},{64,96},{80,112},{96,128},{112,144}... | collective-permute-start | bytes 393224 | tf_op jit(solution)/shard_map/ppermute | solution.py:266
  38.5 5.0 %collective-permute-start.1 = (bf16[8,32,256]{2,1,0:T(8,128)(2,1)S(1)}, bf16[8,32,256]{2,1,0:T(8,128)(2,1)S(1)}, u32[]{:S(2)}, u32[]{:S(2)}) collective-permute-start(bf16[8,32,256]{2,1,0:T(8,128)(2,1)S(1)} %get-tuple-element.13), channel_id=1, source_target_pairs={{32,0},{48,16},{64,32},{80,48},{96,64},{112,80},{128,96},{144,112}... | collective-permute-start | bytes 393224 | tf_op jit(solution)/shard_map/ppermute | solution.py:267
  38.8 6.5 %collective-permute-start.2 = (bf16[8,32,256]{2,1,0:T(8,128)(2,1)S(1)}, bf16[8,32,256]{2,1,0:T(8,128)(2,1)S(1)}, u32[]{:S(2)}, u32[]{:S(2)}) collective-permute-start(bf16[8,32,256]{2,1,0:T(8,128)(2,1)S(1)} %get-tuple-element.15), channel_id=1, source_target_pairs={{0,32},{16,48},{32,64},{48,80},{64,96},{80,112},{96,128},{112,144}... | collective-permute-start | bytes 393224 | tf_op jit(solution)/shard_map/ppermute | solution.py:266
  40.5 5.0 %collective-permute-start.3 = (bf16[8,32,256]{2,1,0:T(8,128)(2,1)S(1)}, bf16[8,32,256]{2,1,0:T(8,128)(2,1)S(1)}, u32[]{:S(2)}, u32[]{:S(2)}) collective-permute-start(bf16[8,32,256]{2,1,0:T(8,128)(2,1)S(1)} %get-tuple-element.16), channel_id=1, source_target_pairs={{32,0},{48,16},{64,32},{80,48},{96,64},{112,80},{128,96},{144,112}... | collective-permute-start | bytes 393224 | tf_op jit(solution)/shard_map/ppermute | solution.py:267

commit v6 on v5

--- a/solution.py
+++ b/solution.py
@@ -9,13 +9,13 @@
 
 STEPS = 8
 LANES = 128
-THERE = (1, 4, 6, 12, 2, 8, 11, 14, 0, 10, 9, 13, 3, 7, 5, 15)
-BACK = (1, 7, 6, 12, 2, 8, 11, 14, 0, 10, 9, 13, 3, 4, 5, 15)
+THERE = (15, 10, 8, 2, 12, 6, 5, 0, 14, 4, 9, 11, 13, 7, 3, 1)
+BACK = (15, 10, 8, 2, 12, 6, 5, 0, 14, 4, 7, 3, 13, 9, 11, 1)
 SPLITS = 2
 
 
 def place(piece, shard, pieces):
-    return piece + (shard % 2) * (pieces - 1 - 2 * piece)
+    return piece + ((shard + 1) % 2) * (pieces - 1 - 2 * piece)
 
 
 def loop_pairs(groups, shards, members):
@@ -55,26 +55,34 @@
     return jnp.where(lax.axis_index("lon") % 2 == 0, ordered(0), ordered(1))
 
 
-def pack_kernel(pieces, field_ref, out_ref):
+def pack_kernel(pieces, field_ref, out_ref, held_ref, sems):
     members, levels, lons, lats = field_ref.shape
     width = lons // pieces
-    for level in range(levels):
-        for member in range(members):
-            for piece in range(pieces):
-                to = slot(THERE, member, piece, members)
+    copies = []
+    for member in range(members):
+        for piece in range(pieces):
+            to = slot(THERE, member, piece, members)
+            for level in range(levels):
                 for half in range(lats // LANES):
                     row = (half * levels + level) * width
                     columns = slice(half * LANES, (half + 1) * LANES)
-                    out_ref[to, row : row + width, :] = field_ref[member, level, piece * width : (piece + 1) * width, columns]
+                    held_ref[to, row : row + width, :] = field_ref[member, level, piece * width : (piece + 1) * width, columns]
+            copy = pltpu.make_async_copy(held_ref.at[to], out_ref.at[to], sems.at[to])
+            copy.start()
+            copies.append(copy)
+    for copy in copies:
+        copy.wait()
 
 
 def pack(field, pieces):
     members, levels, lons, lats = field.shape
+    shape = (pieces * members, levels * (lons // pieces) * lats // LANES, LANES)
     return pl.pallas_call(
         functools.partial(pack_kernel, pieces),
-        out_shape=jax.ShapeDtypeStruct((pieces * members, levels * (lons // pieces) * lats // LANES, LANES), field.dtype),
+        out_shape=jax.ShapeDtypeStruct(shape, field.dtype),
         in_specs=[pl.BlockSpec(memory_space=pltpu.VMEM)],
-        out_specs=pl.BlockSpec(memory_space=pltpu.VMEM),
+        out_specs=pl.BlockSpec(memory_space=pl.ANY),
+        scratch_shapes=[pltpu.VMEM(shape, field.dtype), pltpu.SemaphoreType.DMA((pieces * members,))],
         compiler_params=pltpu.CompilerParams(vmem_limit_bytes=16 * 1024 * 1024),
         name="pack",
     )(field)

time: 79 us -> 78.6 us (level)
  blocking collectives: 29.2 us -> 30.5 us
  starting transfers between devices: 17.2 us -> 16.2 us
    ppermute x2, starting transfers between devices: 4.16 us -> 0.2 us  [on_device(): left = lax.ppermute(tail, ('lev', 'lon'), onward)]
    ppermute x2, starting transfers between devices: 1.21 us -> 4.32 us  [on_device(): right = lax.ppermute(head, ('lev', 'lon'), back)]
    ppermute x2, waiting for transfers between devices: 1.55 us -> 0.01 us  [on_device(): right = lax.ppermute(head, ('lev', 'lon'), back)]
    ppermute x2, waiting for transfers between devices: 0.7 us -> 2.23 us  [on_device(): left = lax.ppermute(tail, ('lev', 'lon'), onward)]
    all_to_all x1, blocking collectives: 29.2 us -> 30.5 us  [exchange(): lax.all_to_all(blocks, ('lev', 'lon'), 0, 0, tiled=True, axis_index_group...]
  transfers between devices with their start and end apart: 5 -> 5, of which waited for: 4 -> 2; matrix products, arithmetic and copies ran while one was open for 3% -> 3% of each run, Pallas kernels for 2% -> 2%
where the time goes in v6:
time: 78.6 us; the launch traced here: 78.2 us
  blocking collectives  30.5 us (39%)
  waiting for transfers between devices  20.2 us (26%)
  starting transfers between devices  16.2 us (21%)
  Pallas kernels  6.74 us (9%)
  local copies, waits for them, and re-layouts  3.89 us (5%)
    all_to_all x1, blocking collectives, exchange(): lax.all_to_all(blocks, ('lev', 'lon'), 0, 0, tiled=True, axis_index_group...  30.5 us
    all_to_all x1, waiting for transfers between devices, exchange(): lax.all_to_all(blocks, ('lev', 'lon'), 0, 0, tiled=True, axis_index_group...  17.9 us
    all_to_all x1, starting transfers between devices, exchange(): lax.all_to_all(blocks, ('lev', 'lon'), 0, 0, tiled=True, axis_index_group...  11.7 us
    ppermute x2, starting transfers between devices, on_device(): right = lax.ppermute(head, ('lev', 'lon'), back)  4.32 us
    pallas_call x2, Pallas kernels, diffused(): pl.pallas_call(diffuse, out_shape=jax.ShapeDtypeStruct(modes.shape, jnp.b...  3.59 us
    unnamed x9, local copies, waits for them, and re-layouts  2.45 us
    ppermute x2, waiting for transfers between devices, on_device(): left = lax.ppermute(tail, ('lev', 'lon'), onward)  2.23 us
  transfers between devices with their start and end apart: 5, of which 2 were waited for; matrix products, arithmetic and copies ran while one was open for 3% of the time, Pallas kernels for 2%

profile of v6, /device:TPU:2, one launch (start us, length us, event | category | flops | bytes accessed | tf_op | source)
XLA Modules:
  0.0 78.2 jit_solution(15406263898405117311)
XLA Ops:
  0.0 1.2 %copy-done = bf16[2,9,96,256]{3,2,1,0:T(8,128)(2,1)S(1)} copy-done((bf16[2,9,96,256]{3,2,1,0:T(8,128)(2,1)S(1)}, bf16[2,9,96,256]{3,2,1,0:T(8,128)(2,1)}, u32[]{:S(2)}) %copy-start) | copy-done | bytes 884760
  1.2 1.1 %pack.1 = bf16[16,216,128]{2,1,0:T(8,128)(2,1)} custom-call(bf16[2,9,96,256]{3,2,1,0:T(8,128)(2,1)S(1)} %copy-done), custom_call_target="tpu_custom_call" | custom-call | tf_op jit(solution)/shard_map/pack/pallas_call | solution.py:80
  2.2 0.0 copy-start.1
  2.2 11.7 %all-to-all-start = ((bf16[16,216,128]{2,1,0:T(8,128)(2,1)}), bf16[16,216,128]{2,1,0:T(8,128)(2,1)S(1)}, u32[]{:S(2)}, u32[]{:S(2)}) async-start(bf16[16,216,128]{2,1,0:T(8,128)(2,1)} %pack.1), calls=%async_computation | async-start | bytes 1769472 | tf_op jit(solution)/shard_map/all_to_all | solution.py:45
  13.9 0.1 fusion.4
  14.1 0.2 concatenate.14
  14.2 0.2 concatenate.15
  14.4 0.2 concatenate.12
  14.6 0.2 concatenate.13
  14.8 0.1 copy.9
  14.9 0.1 copy.8
  15.1 0.3 broadcast_multiply_fusion
  15.4 0.1 mul.37.basis_ref
  15.5 0.1 mul.40
  15.6 0.0 copy-start.2
  15.6 0.1 copy.10
  15.8 0.6 copy-done.2
  16.3 0.1 copy.11
  16.5 0.1 copy.12
  16.5 0.6 copy-done.3
  17.1 0.2 fusion
  17.3 17.9 %all-to-all-done.blocks_ref = bf16[16,216,128]{2,1,0:T(8,128)(2,1)S(1)} async-done(((bf16[16,216,128]{2,1,0:T(8,128)(2,1)}), bf16[16,216,128]{2,1,0:T(8,128)(2,1)S(1)}, u32[]{:S(2)}, u32[]{:S(2)}) %all-to-all-start) | async-done | bytes 884768 | tf_op jit(solution)/shard_map/all_to_all | solution.py:45
  35.3 0.6 project.1
  35.9 0.2 collective-permute-start
  36.1 2.3 %collective-permute-start.1 = (bf16[8,32,256]{2,1,0:T(8,128)(2,1)S(1)}, bf16[8,32,256]{2,1,0:T(8,128)(2,1)S(1)}, u32[]{:S(2)}, u32[]{:S(2)}) collective-permute-start(bf16[8,32,256]{2,1,0:T(8,128)(2,1)S(1)} %get-tuple-element.13), channel_id=1, source_target_pairs={{192,224},{208,240},{160,192},{176,208},{128,160},{144,176},{96,12... | collective-permute-start | bytes 393224 | tf_op jit(solution)/shard_map/ppermute | solution.py:275
  38.4 2.0 %collective-permute-start.3 = (bf16[8,32,256]{2,1,0:T(8,128)(2,1)S(1)}, bf16[8,32,256]{2,1,0:T(8,128)(2,1)S(1)}, u32[]{:S(2)}, u32[]{:S(2)}) collective-permute-start(bf16[8,32,256]{2,1,0:T(8,128)(2,1)S(1)} %get-tuple-element.16), channel_id=1, source_target_pairs={{192,224},{208,240},{160,192},{176,208},{128,160},{144,176},{96,12... | collective-permute-start | bytes 393224 | tf_op jit(solution)/shard_map/ppermute | solution.py:275
  40.4 2.2 %collective-permute-done.left_ref = bf16[8,32,256]{2,1,0:T(8,128)(2,1)S(1)} collective-permute-done((bf16[8,32,256]{2,1,0:T(8,128)(2,1)S(1)}, bf16[8,32,256]{2,1,0:T(8,128)(2,1)S(1)}, u32[]{:S(2)}, u32[]{:S(2)}) %collective-permute-start) | collective-permute-done | bytes 131104 | tf_op jit(solution)/shard_map/ppermute | solution.py:274
  42.6 1.8 %diffuse.2.refs_0_ = bf16[12,32,256]{2,1,0:T(8,128)(2,1)S(1)} custom-call(bf16[12,32,256]{2,1,0:T(8,128)(2,1)S(1)} %get-tuple-element.11.modes_ref, bf16[8,32,256]{2,1,0:T(8,128)(2,1)S(1)} %collective-permute-done.left_ref, bf16[8,32,256]{2,1,0:T(8,128)(2,1)S(1)} %collective-permute-done.1.right_ref, f32[32,256]{1,0:T(8,128)S(1)} %get-tuple-element.18.kappa_ref), custom_call_target="tpu_custom_call" | custom-call | flops 9830400 | bytes 589824 | tf_op jit(solution)/shard_map/diffuse/pallas_call | solution.py:242
  44.4 1.8 %diffuse.3.refs_1_ = bf16[12,32,256]{2,1,0:T(8,128)(2,1)S(1)} custom-call(bf16[12,32,256]{2,1,0:T(8,128)(2,1)S(1)} %get-tuple-element.14.modes_ref, bf16[8,32,256]{2,1,0:T(8,128)(2,1)S(1)} %collective-permute-done.2.left_ref, bf16[8,32,256]{2,1,0:T(8,128)(2,1)S(1)} %collective-permute-done.3.right_ref, f32[32,256]{1,0:T(8,128)S(1)} %get-tuple-element.17.kappa_ref), custom_call_target="tpu_custom_call" | custom-call | flops 9830400 | bytes 589824 | tf_op jit(solution)/shard_map/diffuse/pallas_call | solution.py:242
  46.2 0.5 expand.1
  46.7 30.5 %all_to_all.10.blocks_ref = bf16[16,216,128]{2,1,0:T(8,128)(2,1)S(1)} all-to-all(bf16[16,216,128]{2,1,0:T(8,128)(2,1)S(1)} %expand.1), channel_id=1, replica_groups={{16,64,96,192,32,128,176,224,0,160,144,208,48,112,80,240},{241,161,129,..., dimensions={0} | all-to-all | bytes 1769472 | tf_op jit(solution)/shard_map/all_to_all | solution.py:45
  77.2 1.1 %unpack.1 = bf16[2,9,96,256]{3,2,1,0:T(8,128)(2,1)} custom-call(bf16[16,216,128]{2,1,0:T(8,128)(2,1)S(1)} %all_to_all.10.blocks_ref), custom_call_target="tpu_custom_call" | custom-call | tf_op jit(solution)/shard_map/unpack/pallas_call | solution.py:112
  (12 shorter events, 0.1 us)
Async XLA Ops:
  0.0 1.2 %copy-start = (bf16[2,9,96,256]{3,2,1,0:T(8,128)(2,1)S(1)}, bf16[2,9,96,256]{3,2,1,0:T(8,128)(2,1)}, u32[]{:S(2)}) copy-start(bf16[2,9,96,256]{3,2,1,0:T(8,128)(2,1)} %field_ref.1) | copy-start | bytes 2654212
  2.2 11.7 %copy-start.1 = (bf16[144,64]{0,1:T(8,128)(2,1)S(1)}, bf16[144,64]{0,1:T(8,128)(2,1)}, u32[]{:S(2)}) copy-start(bf16[144,64]{0,1:T(8,128)(2,1)} %param.5) | copy-start | bytes 55300
  2.2 33.0 %all-to-all-start = ((bf16[16,216,128]{2,1,0:T(8,128)(2,1)}), bf16[16,216,128]{2,1,0:T(8,128)(2,1)S(1)}, u32[]{:S(2)}, u32[]{:S(2)}) async-start(bf16[16,216,128]{2,1,0:T(8,128)(2,1)} %pack.1), calls=%async_computation | async-start | bytes 1769472 | tf_op jit(solution)/shard_map/all_to_all | solution.py:45
  15.6 0.7 copy-start.2
  16.5 0.7 copy-start.3
  35.9 6.8 %collective-permute-start = (bf16[8,32,256]{2,1,0:T(8,128)(2,1)S(1)}, bf16[8,32,256]{2,1,0:T(8,128)(2,1)S(1)}, u32[]{:S(2)}, u32[]{:S(2)}) collective-permute-start(bf16[8,32,256]{2,1,0:T(8,128)(2,1)S(1)} %get-tuple-element.12), channel_id=1, source_target_pairs={{224,192},{240,208},{192,160},{208,176},{160,128},{176,144},{128,9... | collective-permute-start | bytes 393224 | tf_op jit(solution)/shard_map/ppermute | solution.py:274
  36.1 6.6 %collective-permute-start.1 = (bf16[8,32,256]{2,1,0:T(8,128)(2,1)S(1)}, bf16[8,32,256]{2,1,0:T(8,128)(2,1)S(1)}, u32[]{:S(2)}, u32[]{:S(2)}) collective-permute-start(bf16[8,32,256]{2,1,0:T(8,128)(2,1)S(1)} %get-tuple-element.13), channel_id=1, source_target_pairs={{192,224},{208,240},{160,192},{176,208},{128,160},{144,176},{96,12... | collective-permute-start | bytes 393224 | tf_op jit(solution)/shard_map/ppermute | solution.py:275
  38.4 6.1 %collective-permute-start.2 = (bf16[8,32,256]{2,1,0:T(8,128)(2,1)S(1)}, bf16[8,32,256]{2,1,0:T(8,128)(2,1)S(1)}, u32[]{:S(2)}, u32[]{:S(2)}) collective-permute-start(bf16[8,32,256]{2,1,0:T(8,128)(2,1)S(1)} %get-tuple-element.15), channel_id=1, source_target_pairs={{224,192},{240,208},{192,160},{208,176},{160,128},{176,144},{128,9... | collective-permute-start | bytes 393224 | tf_op jit(solution)/shard_map/ppermute | solution.py:274
  38.4 6.1 %collective-permute-start.3 = (bf16[8,32,256]{2,1,0:T(8,128)(2,1)S(1)}, bf16[8,32,256]{2,1,0:T(8,128)(2,1)S(1)}, u32[]{:S(2)}, u32[]{:S(2)}) collective-permute-start(bf16[8,32,256]{2,1,0:T(8,128)(2,1)S(1)} %get-tuple-element.16), channel_id=1, source_target_pairs={{192,224},{208,240},{160,192},{176,208},{128,160},{144,176},{96,12... | collective-permute-start | bytes 393224 | tf_op jit(solution)/shard_map/ppermute | solution.py:275

commit v7 on v6

--- a/solution.py
+++ b/solution.py
@@ -9,6 +9,7 @@
 
 STEPS = 8
 LANES = 128
+SPARE = 16
 THERE = (15, 10, 8, 2, 12, 6, 5, 0, 14, 4, 9, 11, 13, 7, 3, 1)
 BACK = (15, 10, 8, 2, 12, 6, 5, 0, 14, 4, 7, 3, 13, 9, 11, 1)
 SPLITS = 2
@@ -156,7 +157,7 @@
         out_shape=shapes * SPLITS,
         in_specs=[pl.BlockSpec(memory_space=pltpu.VMEM)] * 2,
         out_specs=[pl.BlockSpec(memory_space=pltpu.VMEM)] * (3 * SPLITS),
-        scratch_shapes=[pltpu.VMEM((groups * rows, lanes), jnp.float32)],
+        scratch_shapes=[pltpu.VMEM((groups * rows + SPARE, lanes), jnp.float32)],
         compiler_params=pltpu.CompilerParams(vmem_limit_bytes=16 * 1024 * 1024),
         name="project",
     )(blocks, basis)
@@ -183,7 +184,7 @@
         out_shape=jax.ShapeDtypeStruct((groups, rows, lats // 2), jnp.bfloat16),
         in_specs=[pl.BlockSpec(memory_space=pltpu.VMEM)] * (SPLITS + 1),
         out_specs=pl.BlockSpec(memory_space=pltpu.VMEM),
-        scratch_shapes=[pltpu.VMEM((groups * rows, lats // 2), jnp.float32)],
+        scratch_shapes=[pltpu.VMEM((groups * rows + SPARE, lats // 2), jnp.float32)],
         compiler_params=pltpu.CompilerParams(vmem_limit_bytes=16 * 1024 * 1024),
         name="expand",
     )(basis, *parts)

time: 78.6 us -> 78.6 us (level)
  no operation moved by 1% of the time
where the time goes in v7:
time: 78.6 us; the launch traced here: 78.2 us
  blocking collectives  30.5 us (39%)
  waiting for transfers between devices  20.2 us (26%)
  starting transfers between devices  16.2 us (21%)
  Pallas kernels  6.74 us (9%)
  local copies, waits for them, and re-layouts  3.89 us (5%)
    all_to_all x1, blocking collectives, exchange(): lax.all_to_all(blocks, ('lev', 'lon'), 0, 0, tiled=True, axis_index_group...  30.5 us
    all_to_all x1, waiting for transfers between devices, exchange(): lax.all_to_all(blocks, ('lev', 'lon'), 0, 0, tiled=True, axis_index_group...  17.9 us
    all_to_all x1, starting transfers between devices, exchange(): lax.all_to_all(blocks, ('lev', 'lon'), 0, 0, tiled=True, axis_index_group...  11.7 us
    ppermute x2, starting transfers between devices, on_device(): right = lax.ppermute(head, ('lev', 'lon'), back)  4.32 us
    pallas_call x2, Pallas kernels, diffused(): pl.pallas_call(diffuse, out_shape=jax.ShapeDtypeStruct(modes.shape, jnp.b...  3.59 us
    unnamed x9, local copies, waits for them, and re-layouts  2.45 us
    ppermute x2, waiting for transfers between devices, on_device(): left = lax.ppermute(tail, ('lev', 'lon'), onward)  2.23 us
  transfers between devices with their start and end apart: 5, of which 2 were waited for; matrix products, arithmetic and copies ran while one was open for 3% of the time, Pallas kernels for 2%

profile of v7, /device:TPU:2, one launch (start us, length us, event | category | flops | bytes accessed | tf_op | source)
XLA Modules:
  0.0 78.2 jit_solution(10796843598768442050)
XLA Ops:
  0.0 1.2 %copy-done = bf16[2,9,96,256]{3,2,1,0:T(8,128)(2,1)S(1)} copy-done((bf16[2,9,96,256]{3,2,1,0:T(8,128)(2,1)S(1)}, bf16[2,9,96,256]{3,2,1,0:T(8,128)(2,1)}, u32[]{:S(2)}) %copy-start) | copy-done | bytes 884760
  1.2 1.1 %pack.1 = bf16[16,216,128]{2,1,0:T(8,128)(2,1)} custom-call(bf16[2,9,96,256]{3,2,1,0:T(8,128)(2,1)S(1)} %copy-done), custom_call_target="tpu_custom_call" | custom-call | tf_op jit(solution)/shard_map/pack/pallas_call | solution.py:81
  2.2 0.0 copy-start.1
  2.2 11.7 %all-to-all-start = ((bf16[16,216,128]{2,1,0:T(8,128)(2,1)}), bf16[16,216,128]{2,1,0:T(8,128)(2,1)S(1)}, u32[]{:S(2)}, u32[]{:S(2)}) async-start(bf16[16,216,128]{2,1,0:T(8,128)(2,1)} %pack.1), calls=%async_computation | async-start | bytes 1769472 | tf_op jit(solution)/shard_map/all_to_all | solution.py:46
  13.9 0.1 fusion.4
  14.1 0.2 concatenate.14
  14.2 0.2 concatenate.15
  14.4 0.2 concatenate.12
  14.6 0.2 concatenate.13
  14.8 0.1 copy.9
  14.9 0.1 copy.8
  15.1 0.3 broadcast_multiply_fusion
  15.4 0.1 mul.37.basis_ref
  15.5 0.1 mul.40
  15.6 0.0 copy-start.2
  15.6 0.1 copy.10
  15.8 0.6 copy-done.2
  16.3 0.1 copy.11
  16.5 0.1 copy.12
  16.5 0.6 copy-done.3
  17.1 0.2 fusion
  17.3 17.9 %all-to-all-done.blocks_ref = bf16[16,216,128]{2,1,0:T(8,128)(2,1)S(1)} async-done(((bf16[16,216,128]{2,1,0:T(8,128)(2,1)}), bf16[16,216,128]{2,1,0:T(8,128)(2,1)S(1)}, u32[]{:S(2)}, u32[]{:S(2)}) %all-to-all-start) | async-done | bytes 884768 | tf_op jit(solution)/shard_map/all_to_all | solution.py:46
  35.3 0.6 project.1
  35.9 0.2 collective-permute-start
  36.1 2.3 %collective-permute-start.1 = (bf16[8,32,256]{2,1,0:T(8,128)(2,1)S(1)}, bf16[8,32,256]{2,1,0:T(8,128)(2,1)S(1)}, u32[]{:S(2)}, u32[]{:S(2)}) collective-permute-start(bf16[8,32,256]{2,1,0:T(8,128)(2,1)S(1)} %get-tuple-element.13), channel_id=1, source_target_pairs={{192,224},{208,240},{160,192},{176,208},{128,160},{144,176},{96,12... | collective-permute-start | bytes 393224 | tf_op jit(solution)/shard_map/ppermute | solution.py:276
  38.4 2.0 %collective-permute-start.3 = (bf16[8,32,256]{2,1,0:T(8,128)(2,1)S(1)}, bf16[8,32,256]{2,1,0:T(8,128)(2,1)S(1)}, u32[]{:S(2)}, u32[]{:S(2)}) collective-permute-start(bf16[8,32,256]{2,1,0:T(8,128)(2,1)S(1)} %get-tuple-element.16), channel_id=1, source_target_pairs={{192,224},{208,240},{160,192},{176,208},{128,160},{144,176},{96,12... | collective-permute-start | bytes 393224 | tf_op jit(solution)/shard_map/ppermute | solution.py:276
  40.4 2.2 %collective-permute-done.left_ref = bf16[8,32,256]{2,1,0:T(8,128)(2,1)S(1)} collective-permute-done((bf16[8,32,256]{2,1,0:T(8,128)(2,1)S(1)}, bf16[8,32,256]{2,1,0:T(8,128)(2,1)S(1)}, u32[]{:S(2)}, u32[]{:S(2)}) %collective-permute-start) | collective-permute-done | bytes 131104 | tf_op jit(solution)/shard_map/ppermute | solution.py:275
  42.6 1.8 %diffuse.2.refs_0_ = bf16[12,32,256]{2,1,0:T(8,128)(2,1)S(1)} custom-call(bf16[12,32,256]{2,1,0:T(8,128)(2,1)S(1)} %get-tuple-element.11.modes_ref, bf16[8,32,256]{2,1,0:T(8,128)(2,1)S(1)} %collective-permute-done.left_ref, bf16[8,32,256]{2,1,0:T(8,128)(2,1)S(1)} %collective-permute-done.1.right_ref, f32[32,256]{1,0:T(8,128)S(1)} %get-tuple-element.18.kappa_ref), custom_call_target="tpu_custom_call" | custom-call | flops 9830400 | bytes 589824 | tf_op jit(solution)/shard_map/diffuse/pallas_call | solution.py:243
  44.4 1.8 %diffuse.3.refs_1_ = bf16[12,32,256]{2,1,0:T(8,128)(2,1)S(1)} custom-call(bf16[12,32,256]{2,1,0:T(8,128)(2,1)S(1)} %get-tuple-element.14.modes_ref, bf16[8,32,256]{2,1,0:T(8,128)(2,1)S(1)} %collective-permute-done.2.left_ref, bf16[8,32,256]{2,1,0:T(8,128)(2,1)S(1)} %collective-permute-done.3.right_ref, f32[32,256]{1,0:T(8,128)S(1)} %get-tuple-element.17.kappa_ref), custom_call_target="tpu_custom_call" | custom-call | flops 9830400 | bytes 589824 | tf_op jit(solution)/shard_map/diffuse/pallas_call | solution.py:243
  46.2 0.5 expand.1
  46.7 30.5 %all_to_all.10.blocks_ref = bf16[16,216,128]{2,1,0:T(8,128)(2,1)S(1)} all-to-all(bf16[16,216,128]{2,1,0:T(8,128)(2,1)S(1)} %expand.1), channel_id=1, replica_groups={{16,64,96,192,32,128,176,224,0,160,144,208,48,112,80,240},{241,161,129,..., dimensions={0} | all-to-all | bytes 1769472 | tf_op jit(solution)/shard_map/all_to_all | solution.py:46
  77.2 1.1 %unpack.1 = bf16[2,9,96,256]{3,2,1,0:T(8,128)(2,1)} custom-call(bf16[16,216,128]{2,1,0:T(8,128)(2,1)S(1)} %all_to_all.10.blocks_ref), custom_call_target="tpu_custom_call" | custom-call | tf_op jit(solution)/shard_map/unpack/pallas_call | solution.py:113
  (12 shorter events, 0.1 us)
Async XLA Ops:
  0.0 1.2 %copy-start = (bf16[2,9,96,256]{3,2,1,0:T(8,128)(2,1)S(1)}, bf16[2,9,96,256]{3,2,1,0:T(8,128)(2,1)}, u32[]{:S(2)}) copy-start(bf16[2,9,96,256]{3,2,1,0:T(8,128)(2,1)} %field_ref.1) | copy-start | bytes 2654212
  2.2 11.7 %copy-start.1 = (bf16[144,64]{0,1:T(8,128)(2,1)S(1)}, bf16[144,64]{0,1:T(8,128)(2,1)}, u32[]{:S(2)}) copy-start(bf16[144,64]{0,1:T(8,128)(2,1)} %param.5) | copy-start | bytes 55300
  2.2 33.0 %all-to-all-start = ((bf16[16,216,128]{2,1,0:T(8,128)(2,1)}), bf16[16,216,128]{2,1,0:T(8,128)(2,1)S(1)}, u32[]{:S(2)}, u32[]{:S(2)}) async-start(bf16[16,216,128]{2,1,0:T(8,128)(2,1)} %pack.1), calls=%async_computation | async-start | bytes 1769472 | tf_op jit(solution)/shard_map/all_to_all | solution.py:46
  15.6 0.7 copy-start.2
  16.5 0.7 copy-start.3
  35.9 6.8 %collective-permute-start = (bf16[8,32,256]{2,1,0:T(8,128)(2,1)S(1)}, bf16[8,32,256]{2,1,0:T(8,128)(2,1)S(1)}, u32[]{:S(2)}, u32[]{:S(2)}) collective-permute-start(bf16[8,32,256]{2,1,0:T(8,128)(2,1)S(1)} %get-tuple-element.12), channel_id=1, source_target_pairs={{224,192},{240,208},{192,160},{208,176},{160,128},{176,144},{128,9... | collective-permute-start | bytes 393224 | tf_op jit(solution)/shard_map/ppermute | solution.py:275
  36.1 6.6 %collective-permute-start.1 = (bf16[8,32,256]{2,1,0:T(8,128)(2,1)S(1)}, bf16[8,32,256]{2,1,0:T(8,128)(2,1)S(1)}, u32[]{:S(2)}, u32[]{:S(2)}) collective-permute-start(bf16[8,32,256]{2,1,0:T(8,128)(2,1)S(1)} %get-tuple-element.13), channel_id=1, source_target_pairs={{192,224},{208,240},{160,192},{176,208},{128,160},{144,176},{96,12... | collective-permute-start | bytes 393224 | tf_op jit(solution)/shard_map/ppermute | solution.py:276
  38.4 6.1 %collective-permute-start.2 = (bf16[8,32,256]{2,1,0:T(8,128)(2,1)S(1)}, bf16[8,32,256]{2,1,0:T(8,128)(2,1)S(1)}, u32[]{:S(2)}, u32[]{:S(2)}) collective-permute-start(bf16[8,32,256]{2,1,0:T(8,128)(2,1)S(1)} %get-tuple-element.15), channel_id=1, source_target_pairs={{224,192},{240,208},{192,160},{208,176},{160,128},{176,144},{128,9... | collective-permute-start | bytes 393224 | tf_op jit(solution)/shard_map/ppermute | solution.py:275
  38.4 6.1 %collective-permute-start.3 = (bf16[8,32,256]{2,1,0:T(8,128)(2,1)S(1)}, bf16[8,32,256]{2,1,0:T(8,128)(2,1)S(1)}, u32[]{:S(2)}, u32[]{:S(2)}) collective-permute-start(bf16[8,32,256]{2,1,0:T(8,128)(2,1)S(1)} %get-tuple-element.16), channel_id=1, source_target_pairs={{192,224},{208,240},{160,192},{176,208},{128,160},{144,176},{96,12... | collective-permute-start | bytes 393224 | tf_op jit(solution)/shard_map/ppermute | solution.py:276

commit v8 on v7

--- a/solution.py
+++ b/solution.py
@@ -201,55 +201,99 @@
     return spread, gather
 
 
-def diffuse(modes_ref, left_ref, right_ref, kappa_ref, out_ref, u_ref, v_ref):
+def update(get, put, kappa, keep, level, columns, half):
+    lane = lax.broadcasted_iota(jnp.int32, kappa[0].shape, 1)
+    first, last = lane == 0, lane == half - 1
+    for column in columns:
+        before, (even, odd), after = get(level, column - 1), get(level, column), get(level, column + 1)
+        beside_even = odd + jnp.where(first, 0.0, pltpu.roll(odd, 1, 1))
+        beside_odd = even + jnp.where(last, 0.0, pltpu.roll(even, half - 1, 1))
+        put(level + 1, column, 0, keep[0] * even + kappa[0] * ((before[0] + after[0]) + beside_even))
+        put(level + 1, column, 1, keep[1] * odd + kappa[1] * ((before[1] + after[1]) + beside_odd))
+
+
+def coefficients(kappa_ref, half):
+    kappa = kappa_ref[:, :half], kappa_ref[:, half:]
+    return kappa, (1.0 - 4.0 * kappa[0], 1.0 - 4.0 * kappa[1])
+
+
+def inner_kernel(modes_ref, kappa_ref, inner_ref):
     width, count, lats = modes_ref.shape
+    half = lats // 2
+    spread, _ = paired(lats)
+    cells = jnp.dot(modes_ref[...].reshape(width * count, lats), spread, preferred_element_type=jnp.float32)
+    inner_ref[0] = cells.reshape(width, count, lats)
+    kappa, keep = coefficients(kappa_ref, half)
+
+    def get(level, column):
+        return inner_ref[level, column, :, :half], inner_ref[level, column, :, half:]
+
+    def put(level, column, side, value):
+        inner_ref[level, column, :, side * half : (side + 1) * half] = value
+
+    for level in range(inner_ref.shape[0] - 1):
+        update(get, put, kappa, keep, level, range(level + 1, width - level - 1), half)
+
+
+def outer_kernel(inner_ref, left_ref, right_ref, kappa_ref, out_ref, u_ref, v_ref):
+    levels, width, count, lats = inner_ref.shape
     half = lats // 2
     total = width + 2 * STEPS
     spread, gather = paired(lats)
-
-    def load(ref, at):
-        cells = ref[...].reshape(ref.shape[0] * count, lats)
-        cells = jnp.dot(cells, spread, preferred_element_type=jnp.float32)
-        u_ref[at : at + ref.shape[0]] = cells.reshape(ref.shape[0], count, lats)
-
-    load(left_ref, 0)
-    load(modes_ref, STEPS)
-    load(right_ref, STEPS + width)
-    lane = lax.broadcasted_iota(jnp.int32, (count, half), 1)
-    first, last = lane == 0, lane == half - 1
-    kappa = kappa_ref[:, :half], kappa_ref[:, half:]
-    keep = 1.0 - 4.0 * kappa[0], 1.0 - 4.0 * kappa[1]
-    old, new = u_ref, v_ref
-    for step in range(STEPS):
-        before = old[step, :, :half], old[step, :, half:]
-        here = old[step + 1, :, :half], old[step + 1, :, half:]
-        for column in range(step + 1, total - step - 1):
-            after = old[column + 1, :, :half], old[column + 1, :, half:]
-            even, odd = here
-            beside_even = odd + jnp.where(first, 0.0, pltpu.roll(odd, 1, 1))
-            beside_odd = even + jnp.where(last, 0.0, pltpu.roll(even, half - 1, 1))
-            new[column, :, :half] = keep[0] * even + kappa[0] * ((before[0] + after[0]) + beside_even)
-            new[column, :, half:] = keep[1] * odd + kappa[1] * ((before[1] + after[1]) + beside_odd)
-            before, here = here, after
-        old, new = new, old
-    cells = old[STEPS : STEPS + width].astype(jnp.bfloat16).reshape(width * count, lats)
+    for ref, at in ((left_ref, 0), (right_ref, STEPS + width)):
+        cells = jnp.dot(ref[...].reshape(STEPS * count, lats), spread, preferred_element_type=jnp.float32)
+        u_ref[at : at + STEPS] = cells.reshape(STEPS, count, lats)
+    kappa, keep = coefficients(kappa_ref, half)
+
+    def known(level, column):
+        return level < levels and STEPS + level <= column < STEPS + width - level
+
+    def get(level, column):
+        if known(level, column):
+            return inner_ref[level, column - STEPS, :, :half], inner_ref[level, column - STEPS, :, half:]
+        ref = v_ref if level % 2 else u_ref
+        return ref[column, :, :half], ref[column, :, half:]
+
+    def put(level, column, side, value):
+        ref = v_ref if level % 2 else u_ref
+        ref[column, :, side * half : (side + 1) * half] = value
+
+    for level in range(STEPS):
+        columns = [c for c in range(level + 1, total - level - 1) if not known(level + 1, c)]
+        update(get, put, kappa, keep, level, columns, half)
+    final = v_ref if STEPS % 2 else u_ref
+    cells = final[STEPS : STEPS + width].astype(jnp.bfloat16).reshape(width * count, lats)
     cells = jnp.dot(cells, gather, preferred_element_type=jnp.float32)
     out_ref[...] = cells.astype(out_ref.dtype).reshape(width, count, lats)
 
 
-def diffused(modes, left, right, kappa):
+def inner(modes, kappa):
     width, count, lats = modes.shape
+    levels = min((width - 1) // 2, STEPS - 1) + 1
+    return pl.pallas_call(
+        inner_kernel,
+        out_shape=jax.ShapeDtypeStruct((levels, width, count, lats), jnp.float32),
+        in_specs=[pl.BlockSpec(memory_space=pltpu.VMEM)] * 2,
+        out_specs=pl.BlockSpec(memory_space=pltpu.VMEM),
+        compiler_params=pltpu.CompilerParams(vmem_limit_bytes=16 * 1024 * 1024),
+        cost_estimate=pl.CostEstimate(flops=16 * count * lats * width, bytes_accessed=6 * count * lats * width, transcendentals=0),
+        name="inner",
+    )(modes, kappa)
+
+
+def diffused(known, left, right, kappa):
+    levels, width, count, lats = known.shape
     cells = pltpu.VMEM((width + 2 * STEPS, count, lats), jnp.float32)
     return pl.pallas_call(
-        diffuse,
-        out_shape=jax.ShapeDtypeStruct(modes.shape, jnp.bfloat16),
+        outer_kernel,
+        out_shape=jax.ShapeDtypeStruct((width, count, lats), jnp.bfloat16),
         in_specs=[pl.BlockSpec(memory_space=pltpu.VMEM)] * 4,
         out_specs=pl.BlockSpec(memory_space=pltpu.VMEM),
         scratch_shapes=[cells, cells],
         compiler_params=pltpu.CompilerParams(vmem_limit_bytes=16 * 1024 * 1024),
         cost_estimate=pl.CostEstimate(flops=60 * count * lats * (width + STEPS), bytes_accessed=6 * count * lats * width, transcendentals=0),
         name="diffuse",
-    )(modes, left, right, kappa)
+    )(known, left, right, kappa)
 
 
 def on_device(field, eof_basis, band_of_mode, coef_table):
@@ -274,7 +318,8 @@
         some, tail, head = modes[3 * split : 3 * split + 3]
         left = lax.ppermute(tail, ("lev", "lon"), onward)
         right = lax.ppermute(head, ("lev", "lon"), back)
-        parts.append(diffused(some, left, right, kappa[split * share : (split + 1) * share]))
+        some_kappa = kappa[split * share : (split + 1) * share]
+        parts.append(diffused(inner(some, some_kappa), left, right, some_kappa))
     total = expand(parts, doubled(basis_back, groups), groups)
     total = exchange(BACK, total, groups, shards, members)
     return unpack(total, field.shape, pieces)

time: 78.6 us -> 78.2 us (level)
  local copies, waits for them, and re-layouts: 3.89 us -> 2.74 us
    unnamed x9, local copies, waits for them, and re-layouts: 2.45 us -> 1.3 us
    all_to_all x1, waiting for transfers between devices: 17.9 us -> 19.1 us  [exchange(): lax.all_to_all(blocks, ('lev', 'lon'), 0, 0, tiled=True, axis_index_group...]
    ppermute x2, waiting for transfers between devices: 2.23 us -> 1.22 us  [on_device(): left = lax.ppermute(tail, ('lev', 'lon'), onward)]
    pallas_call x2 -> x4, Pallas kernels: 3.59 us -> 4.24 us  [the longest x2 3 us: diffused(): pl.pallas_call(outer_kernel, out_shape=jax.ShapeDtypeStruct((width, count...]
  transfers between devices with their start and end apart: 5 -> 5, of which waited for: 2 -> 3; matrix products, arithmetic and copies ran while one was open for 3% -> 3% of each run, Pallas kernels for 2% -> 4%
where the time goes in v8:
time: 78.2 us; the launch traced here: 78 us
  blocking collectives  30.5 us (39%)
  waiting for transfers between devices  20.3 us (26%)
  starting transfers between devices  16.2 us (21%)
  Pallas kernels  7.38 us (9%)
  local copies, waits for them, and re-layouts  2.74 us (4%)
    all_to_all x1, blocking collectives, exchange(): lax.all_to_all(blocks, ('lev', 'lon'), 0, 0, tiled=True, axis_index_group...  30.5 us
    all_to_all x1, waiting for transfers between devices, exchange(): lax.all_to_all(blocks, ('lev', 'lon'), 0, 0, tiled=True, axis_index_group...  19.1 us
    all_to_all x1, starting transfers between devices, exchange(): lax.all_to_all(blocks, ('lev', 'lon'), 0, 0, tiled=True, axis_index_group...  11.7 us
    ppermute x2, starting transfers between devices, on_device(): right = lax.ppermute(head, ('lev', 'lon'), back)  4.32 us
    pallas_call x2, Pallas kernels, diffused(): pl.pallas_call(outer_kernel, out_shape=jax.ShapeDtypeStruct((width, count...  3 us
  transfers between devices with their start and end apart: 5, of which 3 were waited for; matrix products, arithmetic and copies ran while one was open for 3% of the time, Pallas kernels for 4%

profile of v8, /device:TPU:2, one launch (start us, length us, event | category | flops | bytes accessed | tf_op | source)
XLA Modules:
  0.0 78.0 jit_solution(11817021385988139570)
XLA Ops:
  0.0 1.2 %copy-done = bf16[2,9,96,256]{3,2,1,0:T(8,128)(2,1)S(1)} copy-done((bf16[2,9,96,256]{3,2,1,0:T(8,128)(2,1)S(1)}, bf16[2,9,96,256]{3,2,1,0:T(8,128)(2,1)}, u32[]{:S(2)}) %copy-start) | copy-done | bytes 884760
  1.2 1.1 %pack.1 = bf16[16,216,128]{2,1,0:T(8,128)(2,1)} custom-call(bf16[2,9,96,256]{3,2,1,0:T(8,128)(2,1)S(1)} %copy-done), custom_call_target="tpu_custom_call" | custom-call | tf_op jit(solution)/shard_map/pack/pallas_call | solution.py:81
  2.2 0.0 copy-start.3
  2.2 11.7 %all-to-all-start = ((bf16[16,216,128]{2,1,0:T(8,128)(2,1)}), bf16[16,216,128]{2,1,0:T(8,128)(2,1)S(1)}, u32[]{:S(2)}, u32[]{:S(2)}) async-start(bf16[16,216,128]{2,1,0:T(8,128)(2,1)} %pack.1), calls=%async_computation | async-start | bytes 1769472 | tf_op jit(solution)/shard_map/all_to_all | solution.py:46
  13.9 0.1 fusion.4
  14.1 0.2 concatenate.15
  14.2 0.2 concatenate.14
  14.4 0.2 concatenate.13
  14.6 0.2 concatenate.12
  14.7 0.1 copy.11
  14.9 0.1 copy.12
  15.0 0.1 copy.9
  15.1 0.1 copy.8
  15.3 0.3 broadcast_multiply_fusion
  15.6 0.1 mul.40
  15.7 0.1 copy.10
  15.8 0.1 mul.37.basis_ref
  16.0 0.2 fusion
  16.2 19.1 %all-to-all-done.blocks_ref = bf16[16,216,128]{2,1,0:T(8,128)(2,1)S(1)} async-done(((bf16[16,216,128]{2,1,0:T(8,128)(2,1)}), bf16[16,216,128]{2,1,0:T(8,128)(2,1)S(1)}, u32[]{:S(2)}, u32[]{:S(2)}) %all-to-all-start) | async-done | bytes 884768 | tf_op jit(solution)/shard_map/all_to_all | solution.py:46
  35.3 0.6 project.1
  35.9 0.2 collective-permute-start
  36.1 2.3 %collective-permute-start.1 = (bf16[8,32,256]{2,1,0:T(8,128)(2,1)S(1)}, bf16[8,32,256]{2,1,0:T(8,128)(2,1)S(1)}, u32[]{:S(2)}, u32[]{:S(2)}) collective-permute-start(bf16[8,32,256]{2,1,0:T(8,128)(2,1)S(1)} %get-tuple-element.13), channel_id=1, source_target_pairs={{192,224},{208,240},{160,192},{176,208},{128,160},{144,176},{96,12... | collective-permute-start | bytes 393224 | tf_op jit(solution)/shard_map/ppermute | solution.py:320
  38.4 2.0 %collective-permute-start.3 = (bf16[8,32,256]{2,1,0:T(8,128)(2,1)S(1)}, bf16[8,32,256]{2,1,0:T(8,128)(2,1)S(1)}, u32[]{:S(2)}, u32[]{:S(2)}) collective-permute-start(bf16[8,32,256]{2,1,0:T(8,128)(2,1)S(1)} %get-tuple-element.16), channel_id=1, source_target_pairs={{192,224},{208,240},{160,192},{176,208},{128,160},{144,176},{96,12... | collective-permute-start | bytes 393224 | tf_op jit(solution)/shard_map/ppermute | solution.py:320
  40.4 0.6 inner.2.inner_ref
  41.0 0.6 inner.3.inner_ref
  41.7 1.0 %collective-permute-done.left_ref = bf16[8,32,256]{2,1,0:T(8,128)(2,1)S(1)} collective-permute-done((bf16[8,32,256]{2,1,0:T(8,128)(2,1)S(1)}, bf16[8,32,256]{2,1,0:T(8,128)(2,1)S(1)}, u32[]{:S(2)}, u32[]{:S(2)}) %collective-permute-start) | collective-permute-done | bytes 131104 | tf_op jit(solution)/shard_map/ppermute | solution.py:319
  42.6 1.5 %diffuse.2.refs_0_ = bf16[12,32,256]{2,1,0:T(8,128)(2,1)S(1)} custom-call(f32[6,12,32,256]{3,2,1,0:T(8,128)S(1)} %inner.2.inner_ref, bf16[8,32,256]{2,1,0:T(8,128)(2,1)S(1)} %collective-permute-done.left_ref, bf16[8,32,256]{2,1,0:T(8,128)(2,1)S(1)} %collective-permute-done.1.right_ref, f32[32,256]{1,0:T(8,128)S(1)} %get-tuple-element.18.kappa_ref), custom_call_target="tpu_custom_call" | custom-call | flops 9830400 | bytes 589824 | tf_op jit(solution)/shard_map/diffuse/pallas_call | solution.py:287
  44.1 0.2 collective-permute-done.2.left_ref
  44.4 1.5 %diffuse.3.refs_1_ = bf16[12,32,256]{2,1,0:T(8,128)(2,1)S(1)} custom-call(f32[6,12,32,256]{3,2,1,0:T(8,128)S(1)} %inner.3.inner_ref, bf16[8,32,256]{2,1,0:T(8,128)(2,1)S(1)} %collective-permute-done.2.left_ref, bf16[8,32,256]{2,1,0:T(8,128)(2,1)S(1)} %collective-permute-done.3.right_ref, f32[32,256]{1,0:T(8,128)S(1)} %get-tuple-element.17.kappa_ref), custom_call_target="tpu_custom_call" | custom-call | flops 9830400 | bytes 589824 | tf_op jit(solution)/shard_map/diffuse/pallas_call | solution.py:287
  45.9 0.4 expand.1
  46.4 30.5 %all_to_all.10.blocks_ref = bf16[16,216,128]{2,1,0:T(8,128)(2,1)S(1)} all-to-all(bf16[16,216,128]{2,1,0:T(8,128)(2,1)S(1)} %expand.1), channel_id=1, replica_groups={{16,64,96,192,32,128,176,224,0,160,144,208,48,112,80,240},{241,161,129,..., dimensions={0} | all-to-all | bytes 1769472 | tf_op jit(solution)/shard_map/all_to_all | solution.py:46
  76.9 1.1 %unpack.1 = bf16[2,9,96,256]{3,2,1,0:T(8,128)(2,1)} custom-call(bf16[16,216,128]{2,1,0:T(8,128)(2,1)S(1)} %all_to_all.10.blocks_ref), custom_call_target="tpu_custom_call" | custom-call | tf_op jit(solution)/shard_map/unpack/pallas_call | solution.py:113
  (14 shorter events, 0.1 us)
Async XLA Ops:
  0.0 1.2 %copy-start = (bf16[2,9,96,256]{3,2,1,0:T(8,128)(2,1)S(1)}, bf16[2,9,96,256]{3,2,1,0:T(8,128)(2,1)}, u32[]{:S(2)}) copy-start(bf16[2,9,96,256]{3,2,1,0:T(8,128)(2,1)} %field_ref.1) | copy-start | bytes 2654212
  1.2 12.8 %copy-start.1 = (bf16[144,64]{0,1:T(8,128)(2,1)S(1)}, bf16[144,64]{0,1:T(8,128)(2,1)}, u32[]{:S(2)}) copy-start(bf16[144,64]{0,1:T(8,128)(2,1)} %param.5) | copy-start | bytes 55300
  1.2 13.6 %copy-start.2 = (f32[8,256]{1,0:T(8,128)S(1)}, f32[8,256]{1,0:T(8,128)}, u32[]{:S(2)}) copy-start(f32[8,256]{1,0:T(8,128)} %param.7) | copy-start | bytes 24580
  2.2 13.7 %copy-start.3 = (s32[64]{0:T(128)S(1)}, s32[64]{0:T(128)}, u32[]{:S(2)}) copy-start(s32[64]{0:T(128)} %param.6) | copy-start | bytes 772
  2.2 33.0 %all-to-all-start = ((bf16[16,216,128]{2,1,0:T(8,128)(2,1)}), bf16[16,216,128]{2,1,0:T(8,128)(2,1)S(1)}, u32[]{:S(2)}, u32[]{:S(2)}) async-start(bf16[16,216,128]{2,1,0:T(8,128)(2,1)} %pack.1), calls=%async_computation | async-start | bytes 1769472 | tf_op jit(solution)/shard_map/all_to_all | solution.py:46
  35.9 6.8 %collective-permute-start = (bf16[8,32,256]{2,1,0:T(8,128)(2,1)S(1)}, bf16[8,32,256]{2,1,0:T(8,128)(2,1)S(1)}, u32[]{:S(2)}, u32[]{:S(2)}) collective-permute-start(bf16[8,32,256]{2,1,0:T(8,128)(2,1)S(1)} %get-tuple-element.12), channel_id=1, source_target_pairs={{224,192},{240,208},{192,160},{208,176},{160,128},{176,144},{128,9... | collective-permute-start | bytes 393224 | tf_op jit(solution)/shard_map/ppermute | solution.py:319
  36.1 6.6 %collective-permute-start.1 = (bf16[8,32,256]{2,1,0:T(8,128)(2,1)S(1)}, bf16[8,32,256]{2,1,0:T(8,128)(2,1)S(1)}, u32[]{:S(2)}, u32[]{:S(2)}) collective-permute-start(bf16[8,32,256]{2,1,0:T(8,128)(2,1)S(1)} %get-tuple-element.13), channel_id=1, source_target_pairs={{192,224},{208,240},{160,192},{176,208},{128,160},{144,176},{96,12... | collective-permute-start | bytes 393224 | tf_op jit(solution)/shard_map/ppermute | solution.py:320
  38.4 6.0 %collective-permute-start.2 = (bf16[8,32,256]{2,1,0:T(8,128)(2,1)S(1)}, bf16[8,32,256]{2,1,0:T(8,128)(2,1)S(1)}, u32[]{:S(2)}, u32[]{:S(2)}) collective-permute-start(bf16[8,32,256]{2,1,0:T(8,128)(2,1)S(1)} %get-tuple-element.15), channel_id=1, source_target_pairs={{224,192},{240,208},{192,160},{208,176},{160,128},{176,144},{128,9... | collective-permute-start | bytes 393224 | tf_op jit(solution)/shard_map/ppermute | solution.py:319
  38.4 6.0 %collective-permute-start.3 = (bf16[8,32,256]{2,1,0:T(8,128)(2,1)S(1)}, bf16[8,32,256]{2,1,0:T(8,128)(2,1)S(1)}, u32[]{:S(2)}, u32[]{:S(2)}) collective-permute-start(bf16[8,32,256]{2,1,0:T(8,128)(2,1)S(1)} %get-tuple-element.16), channel_id=1, source_target_pairs={{192,224},{208,240},{160,192},{176,208},{128,160},{144,176},{96,12... | collective-permute-start | bytes 393224 | tf_op jit(solution)/shard_map/ppermute | solution.py:320

commit v9 on v8

--- a/solution.py
+++ b/solution.py
@@ -10,7 +10,7 @@
 STEPS = 8
 LANES = 128
 SPARE = 16
-THERE = (15, 10, 8, 2, 12, 6, 5, 0, 14, 4, 9, 11, 13, 7, 3, 1)
+THERE = (15, 10, 8, 2, 12, 6, 5, 0, 14, 4, 7, 3, 13, 9, 11, 1)
 BACK = (15, 10, 8, 2, 12, 6, 5, 0, 14, 4, 7, 3, 13, 9, 11, 1)
 SPLITS = 2
 

time: 78.2 us -> 77.6 us (level)
  blocking collectives: 30.5 us -> 29.5 us
    all_to_all x1, blocking collectives: 30.5 us -> 29.5 us  [exchange(): lax.all_to_all(blocks, ('lev', 'lon'), 0, 0, tiled=True, axis_index_group...]
  transfers between devices with their start and end apart: 5 -> 5, of which waited for: 3 -> 2; matrix products, arithmetic and copies ran while one was open for 3% -> 2% of each run, Pallas kernels for 4% -> 4%
where the time goes in v9:
time: 77.6 us; the launch traced here: 76.7 us
  blocking collectives  29.5 us (38%)
  waiting for transfers between devices  20.8 us (27%)
  starting transfers between devices  16.2 us (21%)
  Pallas kernels  7.39 us (10%)
  local copies, waits for them, and re-layouts  2.21 us (3%)
    all_to_all x1, blocking collectives, exchange(): lax.all_to_all(blocks, ('lev', 'lon'), 0, 0, tiled=True, axis_index_group...  29.5 us
    all_to_all x1, waiting for transfers between devices, exchange(): lax.all_to_all(blocks, ('lev', 'lon'), 0, 0, tiled=True, axis_index_group...  19.8 us
    all_to_all x1, starting transfers between devices, exchange(): lax.all_to_all(blocks, ('lev', 'lon'), 0, 0, tiled=True, axis_index_group...  11.7 us
    ppermute x2, starting transfers between devices, on_device(): right = lax.ppermute(head, ('lev', 'lon'), back)  4.45 us
    pallas_call x2, Pallas kernels, diffused(): pl.pallas_call(outer_kernel, out_shape=jax.ShapeDtypeStruct((width, count...  2.99 us
  transfers between devices with their start and end apart: 5, of which 2 were waited for; matrix products, arithmetic and copies ran while one was open for 2% of the time, Pallas kernels for 4%

profile of v9, /device:TPU:2, one launch (start us, length us, event | category | flops | bytes accessed | tf_op | source)
XLA Modules:
  0.0 76.7 jit_solution(1777245276106442474)
XLA Ops:
  0.0 1.2 %copy-done = bf16[2,9,96,256]{3,2,1,0:T(8,128)(2,1)S(1)} copy-done((bf16[2,9,96,256]{3,2,1,0:T(8,128)(2,1)S(1)}, bf16[2,9,96,256]{3,2,1,0:T(8,128)(2,1)}, u32[]{:S(2)}) %copy-start) | copy-done | bytes 884760
  1.2 1.1 %pack.1 = bf16[16,216,128]{2,1,0:T(8,128)(2,1)} custom-call(bf16[2,9,96,256]{3,2,1,0:T(8,128)(2,1)S(1)} %copy-done), custom_call_target="tpu_custom_call" | custom-call | tf_op jit(solution)/shard_map/pack/pallas_call | solution.py:81
  2.2 0.0 copy-start.3
  2.2 11.7 %all-to-all-start = ((bf16[16,216,128]{2,1,0:T(8,128)(2,1)}), bf16[16,216,128]{2,1,0:T(8,128)(2,1)S(1)}, u32[]{:S(2)}, u32[]{:S(2)}) async-start(bf16[16,216,128]{2,1,0:T(8,128)(2,1)} %pack.1), calls=%async_computation | async-start | bytes 1769472 | tf_op jit(solution)/shard_map/all_to_all | solution.py:46
  13.9 0.0 copy-done.1
  13.9 0.1 fusion.4
  14.1 0.2 concatenate.9
  14.2 0.2 concatenate.8
  14.4 0.1 copy.9
  14.6 0.1 copy.10
  14.6 0.1 copy.7
  14.8 0.2 broadcast_multiply_fusion
  15.0 0.1 mul.13.basis_ref
  15.1 0.1 copy.8.basis_ref
  15.3 0.2 fusion
  15.5 19.8 %all-to-all-done.blocks_ref = bf16[16,216,128]{2,1,0:T(8,128)(2,1)S(1)} async-done(((bf16[16,216,128]{2,1,0:T(8,128)(2,1)}), bf16[16,216,128]{2,1,0:T(8,128)(2,1)S(1)}, u32[]{:S(2)}, u32[]{:S(2)}) %all-to-all-start) | async-done | bytes 884768 | tf_op jit(solution)/shard_map/all_to_all | solution.py:46
  35.3 0.6 project.1
  35.9 0.1 collective-permute-start
  36.0 2.4 %collective-permute-start.1 = (bf16[8,32,256]{2,1,0:T(8,128)(2,1)S(1)}, bf16[8,32,256]{2,1,0:T(8,128)(2,1)S(1)}, u32[]{:S(2)}, u32[]{:S(2)}) collective-permute-start(bf16[8,32,256]{2,1,0:T(8,128)(2,1)S(1)} %get-tuple-element.13), channel_id=1, source_target_pairs={{192,224},{208,240},{160,192},{176,208},{128,160},{144,176},{96,12... | collective-permute-start | bytes 393224 | tf_op jit(solution)/shard_map/ppermute | solution.py:320
  38.4 0.0 collective-permute-start.2
  38.4 2.0 %collective-permute-start.3 = (bf16[8,32,256]{2,1,0:T(8,128)(2,1)S(1)}, bf16[8,32,256]{2,1,0:T(8,128)(2,1)S(1)}, u32[]{:S(2)}, u32[]{:S(2)}) collective-permute-start(bf16[8,32,256]{2,1,0:T(8,128)(2,1)S(1)} %get-tuple-element.16), channel_id=1, source_target_pairs={{192,224},{208,240},{160,192},{176,208},{128,160},{144,176},{96,12... | collective-permute-start | bytes 393224 | tf_op jit(solution)/shard_map/ppermute | solution.py:320
  40.4 0.6 inner.2.inner_ref
  41.0 0.6 inner.3.inner_ref
  41.7 1.0 %collective-permute-done.left_ref = bf16[8,32,256]{2,1,0:T(8,128)(2,1)S(1)} collective-permute-done((bf16[8,32,256]{2,1,0:T(8,128)(2,1)S(1)}, bf16[8,32,256]{2,1,0:T(8,128)(2,1)S(1)}, u32[]{:S(2)}, u32[]{:S(2)}) %collective-permute-start) | collective-permute-done | bytes 131104 | tf_op jit(solution)/shard_map/ppermute | solution.py:319
  42.7 0.0 collective-permute-done.1.right_ref
  42.7 1.5 %diffuse.2.refs_0_ = bf16[12,32,256]{2,1,0:T(8,128)(2,1)S(1)} custom-call(f32[6,12,32,256]{3,2,1,0:T(8,128)S(1)} %inner.2.inner_ref, bf16[8,32,256]{2,1,0:T(8,128)(2,1)S(1)} %collective-permute-done.left_ref, bf16[8,32,256]{2,1,0:T(8,128)(2,1)S(1)} %collective-permute-done.1.right_ref, f32[32,256]{1,0:T(8,128)S(1)} %get-tuple-element.18.kappa_ref), custom_call_target="tpu_custom_call" | custom-call | flops 9830400 | bytes 589824 | tf_op jit(solution)/shard_map/diffuse/pallas_call | solution.py:287
  44.2 0.0 collective-permute-done.2.left_ref
  44.2 0.0 collective-permute-done.3.right_ref
  44.2 1.5 %diffuse.3.refs_1_ = bf16[12,32,256]{2,1,0:T(8,128)(2,1)S(1)} custom-call(f32[6,12,32,256]{3,2,1,0:T(8,128)S(1)} %inner.3.inner_ref, bf16[8,32,256]{2,1,0:T(8,128)(2,1)S(1)} %collective-permute-done.2.left_ref, bf16[8,32,256]{2,1,0:T(8,128)(2,1)S(1)} %collective-permute-done.3.right_ref, f32[32,256]{1,0:T(8,128)S(1)} %get-tuple-element.17.kappa_ref), custom_call_target="tpu_custom_call" | custom-call | flops 9830400 | bytes 589824 | tf_op jit(solution)/shard_map/diffuse/pallas_call | solution.py:287
  45.7 0.4 expand.1
  46.2 29.5 %all_to_all.10.blocks_ref = bf16[16,216,128]{2,1,0:T(8,128)(2,1)S(1)} all-to-all(bf16[16,216,128]{2,1,0:T(8,128)(2,1)S(1)} %expand.1), channel_id=1, replica_groups={{16,64,96,192,32,128,176,224,0,160,144,208,48,112,80,240},{241,161,129,..., dimensions={0} | all-to-all | bytes 1769472 | tf_op jit(solution)/shard_map/all_to_all | solution.py:46
  75.6 1.1 %unpack.1 = bf16[2,9,96,256]{3,2,1,0:T(8,128)(2,1)} custom-call(bf16[16,216,128]{2,1,0:T(8,128)(2,1)S(1)} %all_to_all.10.blocks_ref), custom_call_target="tpu_custom_call" | custom-call | tf_op jit(solution)/shard_map/unpack/pallas_call | solution.py:113
  (9 shorter events, 0.1 us)
Async XLA Ops:
  0.0 1.2 %copy-start = (bf16[2,9,96,256]{3,2,1,0:T(8,128)(2,1)S(1)}, bf16[2,9,96,256]{3,2,1,0:T(8,128)(2,1)}, u32[]{:S(2)}) copy-start(bf16[2,9,96,256]{3,2,1,0:T(8,128)(2,1)} %field_ref.1) | copy-start | bytes 2654212
  1.2 12.8 %copy-start.1 = (bf16[144,64]{0,1:T(8,128)(2,1)S(1)}, bf16[144,64]{0,1:T(8,128)(2,1)}, u32[]{:S(2)}) copy-start(bf16[144,64]{0,1:T(8,128)(2,1)} %param.5) | copy-start | bytes 55300
  1.2 13.2 %copy-start.2 = (f32[8,256]{1,0:T(8,128)S(1)}, f32[8,256]{1,0:T(8,128)}, u32[]{:S(2)}) copy-start(f32[8,256]{1,0:T(8,128)} %param.7) | copy-start | bytes 24580
  2.2 13.0 %copy-start.3 = (s32[64]{0:T(128)S(1)}, s32[64]{0:T(128)}, u32[]{:S(2)}) copy-start(s32[64]{0:T(128)} %param.6) | copy-start | bytes 772
  2.2 33.0 %all-to-all-start = ((bf16[16,216,128]{2,1,0:T(8,128)(2,1)}), bf16[16,216,128]{2,1,0:T(8,128)(2,1)S(1)}, u32[]{:S(2)}, u32[]{:S(2)}) async-start(bf16[16,216,128]{2,1,0:T(8,128)(2,1)} %pack.1), calls=%async_computation | async-start | bytes 1769472 | tf_op jit(solution)/shard_map/all_to_all | solution.py:46
  35.9 6.8 %collective-permute-start = (bf16[8,32,256]{2,1,0:T(8,128)(2,1)S(1)}, bf16[8,32,256]{2,1,0:T(8,128)(2,1)S(1)}, u32[]{:S(2)}, u32[]{:S(2)}) collective-permute-start(bf16[8,32,256]{2,1,0:T(8,128)(2,1)S(1)} %get-tuple-element.12), channel_id=1, source_target_pairs={{224,192},{240,208},{192,160},{208,176},{160,128},{176,144},{128,9... | collective-permute-start | bytes 393224 | tf_op jit(solution)/shard_map/ppermute | solution.py:319
  36.0 6.7 %collective-permute-start.1 = (bf16[8,32,256]{2,1,0:T(8,128)(2,1)S(1)}, bf16[8,32,256]{2,1,0:T(8,128)(2,1)S(1)}, u32[]{:S(2)}, u32[]{:S(2)}) collective-permute-start(bf16[8,32,256]{2,1,0:T(8,128)(2,1)S(1)} %get-tuple-element.13), channel_id=1, source_target_pairs={{192,224},{208,240},{160,192},{176,208},{128,160},{144,176},{96,12... | collective-permute-start | bytes 393224 | tf_op jit(solution)/shard_map/ppermute | solution.py:320
  38.4 5.8 %collective-permute-start.2 = (bf16[8,32,256]{2,1,0:T(8,128)(2,1)S(1)}, bf16[8,32,256]{2,1,0:T(8,128)(2,1)S(1)}, u32[]{:S(2)}, u32[]{:S(2)}) collective-permute-start(bf16[8,32,256]{2,1,0:T(8,128)(2,1)S(1)} %get-tuple-element.15), channel_id=1, source_target_pairs={{224,192},{240,208},{192,160},{208,176},{160,128},{176,144},{128,9... | collective-permute-start | bytes 393224 | tf_op jit(solution)/shard_map/ppermute | solution.py:319
  38.4 5.8 %collective-permute-start.3 = (bf16[8,32,256]{2,1,0:T(8,128)(2,1)S(1)}, bf16[8,32,256]{2,1,0:T(8,128)(2,1)S(1)}, u32[]{:S(2)}, u32[]{:S(2)}) collective-permute-start(bf16[8,32,256]{2,1,0:T(8,128)(2,1)S(1)} %get-tuple-element.16), channel_id=1, source_target_pairs={{192,224},{208,240},{160,192},{176,208},{128,160},{144,176},{96,12... | collective-permute-start | bytes 393224 | tf_op jit(solution)/shard_map/ppermute | solution.py:320
